TPU v7x, 32 devices: a whole 2x2x4 slice. The times are simulated.
32 devices in a mesh: gx: 4 (over y, x), gy: 8 (over z, core).
Axes of the slice: x: 2, y: 2, z: 4, core: 2. Of those that a mesh axis runs over, the one named last changes fastest.
Arguments:
- field: float32 [3, 16, 256, 1024], P(None, None, 'gx', 'gy'), may hold values from -6 to 6
- masks: int32 [2, 7, 8, 32], P(None, None, 'gx', 'gy'), may hold values 0 or 1
Outputs:
- restored: float32 [3, 16, 256, 1024], P(None, None, 'gx', 'gy')
- coarse: float32 [3, 4, 64, 256], replicated
All inputs are finite; a program needn't handle non-finite values. No bound on the sum of `masks` on one device may be relied on, other than what follows from the above.
Results may differ from a plain program's by a relative error of at most 0.00002.
Values sent between devices are 32-bit elements; how exact they have to be, the bound alone decides.
No kernel may reach another device: no remote copies, remote signals or barrier semaphores. Data moves between devices by JAX's collectives and lax.ppermute only.
A program may use at most 128 MiB of HBM per device.

v0:
```python
import jax
import jax.numpy as jnp
from jax import lax
from jax.sharding import PartitionSpec as P

BLOCK = 32


def extended(x, sides, width):
    for axis, dim in sides:
        count, length = (lax.axis_size(axis), x.shape[dim])
        up = [(i, (i + 1) % count) for i in range(count)]
        down = [(j, i) for i, j in up]
        last = lax.slice_in_dim(x, length - width, length, axis=dim)
        leading = lax.slice_in_dim(x, 0, width, axis=dim)
        before = lax.ppermute(last, axis, up)
        after = lax.ppermute(leading, axis, down)
        x = jnp.concatenate([before, x, after], axis=dim)
    return x


def take_slice(volume, start, stop, stride, direction):
    return lax.slice_in_dim(volume, start, stop, stride, direction)


def lift_forward(padded, direction):
    length = padded.shape[direction] - 4
    even_cells = take_slice(padded, 2, length + 2, 2, direction)
    odd_cells = take_slice(padded, 3, length + 3, 2, direction)
    next_even = take_slice(padded, 4, length + 4, 2, direction)
    detail = odd_cells - 0.5 * (even_cells + next_even)
    first_detail = take_slice(padded, 1, 2, 1, direction) - 0.5 * (
        take_slice(padded, 0, 1, 1, direction) + take_slice(padded, 2, 3, 1, direction)
    )
    previous = jnp.concatenate(
        [first_detail, take_slice(detail, 0, length // 2 - 1, 1, direction)], direction
    )
    smooth = even_cells + 0.25 * (previous + detail)
    return jnp.concatenate([smooth, detail], 0)


def lift_inverse(padded, direction):
    middle = padded.shape[0] // 2
    smooth_pad = padded[:middle]
    detail_pad = padded[middle:]
    length = padded.shape[direction] - 2
    even_ext = take_slice(smooth_pad, 1, length + 2, 1, direction) - 0.25 * (
        take_slice(detail_pad, 0, length + 1, 1, direction)
        + take_slice(detail_pad, 1, length + 2, 1, direction)
    )
    even_cells = take_slice(even_ext, 0, length, 1, direction)
    next_even = take_slice(even_ext, 1, length + 1, 1, direction)
    odd_cells = take_slice(detail_pad, 1, length + 1, 1, direction) + 0.5 * (even_cells + next_even)
    target_shape = list(even_cells.shape)
    target_shape[direction] = 2 * length
    return jnp.stack([even_cells, odd_cells], direction + 1).reshape(target_shape)


def mirror_forward(volume, direction):
    length = volume.shape[direction]
    return jnp.concatenate(
        [
            take_slice(volume, 2, 3, 1, direction),
            take_slice(volume, 1, 2, 1, direction),
            volume,
            take_slice(volume, length - 2, length - 1, 1, direction),
            take_slice(volume, length - 3, length - 2, 1, direction),
        ],
        direction,
    )


def mirror_inverse(volume, direction):
    middle = volume.shape[0] // 2
    length = volume.shape[direction]
    smooth = volume[:middle]
    detail = volume[middle:]
    smooth_pad = jnp.concatenate(
        [
            take_slice(smooth, 0, 1, 1, direction),
            smooth,
            take_slice(smooth, length - 1, length, 1, direction),
        ],
        direction,
    )
    detail_pad = jnp.concatenate(
        [
            take_slice(detail, 0, 1, 1, direction),
            detail,
            take_slice(detail, length - 2, length - 1, 1, direction),
        ],
        direction,
    )
    return jnp.concatenate([smooth_pad, detail_pad], 0)


def expand_mask(mask_block, block_width):
    return jnp.repeat(jnp.repeat(mask_block, block_width, 1), block_width, 2).astype(jnp.float32)


def grid_forward(volume):
    padded = extended(volume, (("gx", 3), ("gy", 4)), 2)
    volume = lift_forward(padded, 3)
    volume = lift_forward(volume, 4)
    return lift_forward(mirror_forward(volume, 2), 2)


def grid_inverse(volume):
    volume = lift_inverse(mirror_inverse(volume, 2), 2)
    padded = extended(volume, (("gx", 3), ("gy", 4)), 1)
    volume = lift_inverse(padded, 4)
    volume = lift_inverse(volume, 3)
    return volume


def gather_coarse(local_coarse):
    partial_rows = lax.all_gather(local_coarse, "gy", axis=3, tiled=True)
    return lax.all_gather(partial_rows, "gx", axis=2, tiled=True)


def body(field, masks):
    coarse = None
    local_coarse = None
    volume = field[None]
    detail_list = []
    volume = grid_forward(volume)
    detail_list.append(volume[1:] * expand_mask(masks[0], BLOCK >> 1)[:, None, None, :, :])
    volume = volume[:1]
    level_index = 1
    volume = grid_forward(volume)
    kept_mask = expand_mask(masks[level_index], BLOCK >> level_index + 1)
    detail_list.append(volume[1:] * kept_mask[:, None, None, :, :])
    volume = volume[:1]
    local_coarse = volume[0]
    level_index = 1
    volume = grid_inverse(jnp.concatenate([volume, detail_list[level_index]], 0))
    volume = grid_inverse(jnp.concatenate([volume, detail_list[0]], 0))
    restored = volume[0]
    coarse = gather_coarse(local_coarse)
    return (restored, coarse)


def solution(mesh):
    placed = (P(None, None, "gx", "gy"), P(None, None, "gx", "gy"))
    return jax.shard_map(
        body,
        mesh=mesh,
        in_specs=placed,
        out_specs=(P(None, None, "gx", "gy"), P()),
        check_vma=False,
    )
```

profile of v0, /device:TPU:0, one launch (start us, length us, event | category | flops | bytes accessed | tf_op | source)
XLA Modules:
  0.0 326.9 jit_solution(7292031643656321503)
XLA Ops:
  13.4 3.6 %collective-permute-start.3 = (f32[1,3,16,68,2]{3,2,4,1,0:T(8,128)S(1)}, f32[1,3,16,68,2]{3,2,4,1,0:T(8,128)S(1)}, u32[]{:S(2)}, u32[]{:S(2)}) collective-permute-start(f32[1,3,16,68,2]{3,2,4,1,0:T(8,128)S(1)} %copy.114), channel_id=1, source_target_pairs={{1,0},{2,1},{3,2},{4,3},{5,4},{6,5},{7,6},{0,7},{9,8},{10,9},{11,1... | collective-permute-start | bytes 78344 | tf_op jit(solution)/shard_map/ppermute | solution.py:17
  22.1 4.2 %pad_maximum_fusion.5 = f32[1,3,16,68,132]{4,3,2,1,0:T(8,128)S(1)} fusion(f32[1,3,16,68,2]{4,3,2,1,0:T(8,128)} %copy.116, f32[1,3,16,2,128]{4,3,2,1,0:T(2,128)} %copy-done.19, f32[1,3,16,64,128]{4,3,2,1,0:T(8,128)} %bitcast.69, f32[1,3,16,2,128]{4,3,2,1,0:T(2,128)} %copy-done.18, f32[1,3,16,68,2]{4,3,2,1,0:T(8,128)} %copy.115), kind=kLoop, calls=%fused_computation.23 | loop fusion | flops 1723392 | bytes 3446784 | tf_op jit(solution)/shard_map/concatenate | solution.py:18
  26.3 4.6 %slice.382 = f32[1,3,16,32,132]{4,3,2,1,0:T(8,128)} slice(f32[1,3,16,68,132]{4,3,2,1,0:T(8,128)S(1)} %pad_maximum_fusion.5), slice={[0:1:1], [0:3:1], [0:16:1], [2:66:2], [0:132:1]} | slice | bytes 1622016 | tf_op jit(solution)/shard_map/slice | solution.py:23
  30.8 4.4 %slice.386 = f32[1,3,16,32,132]{4,3,2,1,0:T(8,128)} slice(f32[1,3,16,68,132]{4,3,2,1,0:T(8,128)S(1)} %pad_maximum_fusion.5), slice={[0:1:1], [0:3:1], [0:16:1], [3:67:2], [0:132:1]} | slice | bytes 1622016 | tf_op jit(solution)/shard_map/slice | solution.py:23
  35.2 4.4 %slice.387 = f32[1,3,16,32,132]{4,3,2,1,0:T(8,128)} slice(f32[1,3,16,68,132]{4,3,2,1,0:T(8,128)S(1)} %pad_maximum_fusion.5), slice={[0:1:1], [0:3:1], [0:16:1], [4:68:2], [0:132:1]} | slice | bytes 1622016 | tf_op jit(solution)/shard_map/slice | solution.py:23
  45.7 36.9 %slice.389 = f32[2,3,16,32,64]{4,3,2,1,0:T(8,128)} slice(f32[2,3,16,32,132]{4,3,2,1,0:T(8,128)S(1)} %pad_maximum_fusion.2), slice={[0:2:1], [0:3:1], [0:16:1], [0:32:1], [2:130:2]} | slice | bytes 1572864 | tf_op jit(solution)/shard_map/slice | solution.py:23
  82.5 36.9 %slice.393 = f32[2,3,16,32,64]{4,3,2,1,0:T(8,128)} slice(f32[2,3,16,32,132]{4,3,2,1,0:T(8,128)S(1)} %pad_maximum_fusion.2), slice={[0:2:1], [0:3:1], [0:16:1], [0:32:1], [3:131:2]} | slice | bytes 1572864 | tf_op jit(solution)/shard_map/slice | solution.py:23
  119.4 36.8 %slice.394 = f32[2,3,16,32,64]{4,3,2,1,0:T(8,128)} slice(f32[2,3,16,32,132]{4,3,2,1,0:T(8,128)S(1)} %pad_maximum_fusion.2), slice={[0:2:1], [0:3:1], [0:16:1], [0:32:1], [4:132:2]} | slice | bytes 1572864 | tf_op jit(solution)/shard_map/slice | solution.py:23
  169.6 3.5 %collective-permute-start.7 = (f32[1,3,8,36,2]{4,3,2,1,0:T(8,128)S(1)}, f32[1,3,8,36,2]{4,3,2,1,0:T(8,128)S(1)}, u32[]{:S(2)}, u32[]{:S(2)}) collective-permute-start(f32[1,3,8,36,2]{4,3,2,1,0:T(8,128)S(1)} %get-tuple-element.57), channel_id=1, source_target_pairs={{1,0},{2,1},{3,2},{4,3},{5,4},{6,5},{7,6},{0,7},{9,8},{10,9},{11,1... | collective-permute-start | bytes 20744 | tf_op jit(solution)/shard_map/ppermute | solution.py:17
  174.3 10.3 %collective-permute-done.6 = f32[1,3,8,36,2]{4,3,2,1,0:T(8,128)S(1)} collective-permute-done((f32[1,3,8,36,2]{4,3,2,1,0:T(8,128)S(1)}, f32[1,3,8,36,2]{4,3,2,1,0:T(8,128)S(1)}, u32[]{:S(2)}, u32[]{:S(2)}) %collective-permute-start.6) | collective-permute-done | bytes 6944 | tf_op jit(solution)/shard_map/ppermute | solution.py:16
  186.2 3.8 %slice.417 = f32[2,3,8,16,32]{4,3,2,1,0:T(8,128)S(1)} slice(f32[2,3,8,16,68]{4,3,2,1,0:T(8,128)S(1)} %pad_maximum_fusion.19), slice={[0:2:1], [0:3:1], [0:8:1], [0:16:1], [2:66:2]} | slice | bytes 196608 | tf_op jit(solution)/shard_map/slice | solution.py:23
  190.0 3.8 %slice.421 = f32[2,3,8,16,32]{4,3,2,1,0:T(8,128)S(1)} slice(f32[2,3,8,16,68]{4,3,2,1,0:T(8,128)S(1)} %pad_maximum_fusion.19), slice={[0:2:1], [0:3:1], [0:8:1], [0:16:1], [3:67:2]} | slice | bytes 196608 | tf_op jit(solution)/shard_map/slice | solution.py:23
  193.8 3.8 %slice.422 = f32[2,3,8,16,32]{4,3,2,1,0:T(8,128)S(1)} slice(f32[2,3,8,16,68]{4,3,2,1,0:T(8,128)S(1)} %pad_maximum_fusion.19), slice={[0:2:1], [0:3:1], [0:8:1], [0:16:1], [4:68:2]} | slice | bytes 196608 | tf_op jit(solution)/shard_map/slice | solution.py:23
  241.6 18.4 %all-gather = f32[1,3,4,16,256]{3,2,1,0,4:T(4,128)} all-gather(f32[1,3,4,16,32]{3,2,1,0,4:T(4,128)S(1)} %copy-done.12), channel_id=2, replica_groups=mesh['gx'=4,'gy'=8] {'gy'}, dimensions={4}, use_global_device_ids=true | all-gather | bytes 221184 | tf_op jit(solution)/shard_map/all_gather | solution.py:117
  262.6 4.4 %fusion.84 = (f32[4,3,16,34,1]{4,3,2,1,0:T(8,128)}, f32[4,3,16,34,1]{4,3,2,1,0:T(8,128)}) fusion(f32[4,3,16,34,64]{4,3,2,1,0:T(8,128)S(1)} %pad_maximum_fusion.3), kind=kLoop, calls=%fused_computation.196 | loop fusion | bytes 104448 | tf_op jit(solution)/shard_map/slice | solution.py:14
  267.0 3.7 %copy.132 = f32[4,3,16,34,1]{3,2,4,1,0:T(8,128)} copy(f32[4,3,16,34,1]{4,3,2,1,0:T(8,128)} %get-tuple-element.13) | data formatting | bytes 52224 | tf_op jit(solution)/shard_map/slice | solution.py:15
  272.2 11.4 %all-gather.1 = f32[1,3,4,64,256]{4,2,1,0,3:T(4,128)S(1)} all-gather(f32[1,3,4,16,256]{4,2,1,0,3:T(4,128)S(1)} %copy.142), channel_id=3, replica_groups=mesh['gx'=4,'gy'=8] {'gx'}, dimensions={3}, use_global_device_ids=true | all-gather | bytes 983040 | tf_op jit(solution)/shard_map/all_gather | solution.py:118
  284.6 3.1 copy.134
  287.8 3.7 %copy.133 = f32[4,3,16,34,1]{4,3,2,1,0:T(8,128)} copy(f32[4,3,16,34,1]{3,2,4,1,0:T(8,128)} %collective-permute-done.14) | data formatting | bytes 52224 | tf_op jit(solution)/shard_map/ppermute | solution.py:17
  291.5 5.2 %pad_maximum_fusion.4 = f32[4,3,16,34,65]{4,3,2,1,0:T(8,128)} fusion(f32[4,3,16,34,1]{4,3,2,1,0:T(8,128)} %copy.133, f32[4,3,16,1,64]{4,3,2,1,0:T(1,128)S(1)} %collective-permute-done.13, f32[4,3,16,32,64]{4,3,2,1,0:T(8,128)S(1)} %bitcast.54, f32[4,3,16,1,64]{4,3,2,1,0:T(1,128)S(1)} %collective-permute-done.12), kind=kLoop, calls=%fused_computation.20 | loop fusion | flops 1272960 | bytes 3394560 | tf_op jit(solution)/shard_map/concatenate | solution.py:18
  299.7 3.8 %fusion.11 = f32[2,3,16,34,65]{4,3,2,1,0:T(8,128)S(1)} fusion(f32[4,3,16,34,65]{4,3,2,1,0:T(8,128)} %pad_maximum_fusion.4, f32[4,3,16,34,1]{4,3,2,1,0:T(8,128)} %copy.135, f32[4,3,16,1,64]{4,3,2,1,0:T(1,128)S(1)} %collective-permute-done.13, f32[4,3,16,32,64]{4,3,2,1,0:T(8,128)S(1)} %bitcast.55, f32[4,3,16,1,64]{4,3,2,1,0:T(1,128)S(1)} %collective-permute-done.12), kind=kLoop, calls=%fused_computation.45 | loop fusion | flops 1272960 | bytes 4243200 | tf_op jit(solution)/shard_map/sub | solution.py:47
  311.4 3.6 %fusion.4 = f32[1,3,16,33,128]{3,2,4,1,0:T(8,128)S(1)} fusion(f32[1,3,16,34,128]{3,2,4,1,0:T(8,128)S(1)} %bitcast.56, f32[1,3,16,34,128]{3,2,4,1,0:T(8,128)} %bitcast.64), kind=kLoop, calls=%fused_computation.30 | loop fusion | flops 608256 | bytes 3244032 | tf_op jit(solution)/shard_map/sub | solution.py:47
  316.7 3.3 %pad_maximum_fusion = f32[1,3,16,32,2,128]{3,2,5,1,4,0:T(8,128)} fusion(f32[1,3,16,32,1,128]{3,2,5,1,4,0:T(8,128)S(1)} %get-tuple-element.15, f32[1,3,16,32,1,128]{3,2,5,1,4,0:T(8,128)S(1)} %get-tuple-element.14), kind=kLoop, calls=%fused_computation | loop fusion | flops 393216 | bytes 3145728 | tf_op jit(solution)/shard_map/stack | solution.py:56
  320.0 5.1 %copy.140 = f32[1,3,16,32,2,128]{5,2,4,3,1,0:T(8,128)S(1)} copy(f32[1,3,16,32,2,128]{3,2,5,1,4,0:T(8,128)} %pad_maximum_fusion) | data formatting | bytes 3145728 | tf_op jit(solution)/shard_map/stack | solution.py:56
  (170 shorter events, 103.0 us)
Async XLA Ops:
  1.7 6.0 %collective-permute-start = (f32[1,3,16,2,128]{4,3,2,1,0:T(2,128)S(1)}, f32[1,3,16,2,128]{4,3,2,1,0:T(2,128)S(1)}, u32[]{:S(2)}, u32[]{:S(2)}) collective-permute-start(f32[1,3,16,2,128]{4,3,2,1,0:T(2,128)S(1)} %get-tuple-element.34), channel_id=1, source_target_pairs={{0,8},{8,16},{16,24},{24,0},{1,9},{9,17},{17,25},{25,1},{2,10},{10... | collective-permute-start | bytes 147464 | tf_op jit(solution)/shard_map/ppermute | solution.py:16
  4.7 4.1 %collective-permute-start.1 = (f32[1,3,16,2,128]{4,3,2,1,0:T(2,128)S(1)}, f32[1,3,16,2,128]{4,3,2,1,0:T(2,128)S(1)}, u32[]{:S(2)}, u32[]{:S(2)}) collective-permute-start(f32[1,3,16,2,128]{4,3,2,1,0:T(2,128)S(1)} %get-tuple-element.35), channel_id=1, source_target_pairs={{8,0},{16,8},{24,16},{0,24},{9,1},{17,9},{25,17},{1,25},{10,2},{18... | collective-permute-start | bytes 147464 | tf_op jit(solution)/shard_map/ppermute | solution.py:17
  12.8 5.5 %collective-permute-start.2 = (f32[1,3,16,68,2]{3,2,4,1,0:T(8,128)}, f32[1,3,16,68,2]{3,2,4,1,0:T(8,128)S(1)}, u32[]{:S(2)}, u32[]{:S(2)}) collective-permute-start(f32[1,3,16,68,2]{3,2,4,1,0:T(8,128)} %copy.113), channel_id=1, source_target_pairs={{0,1},{1,2},{2,3},{3,4},{4,5},{5,6},{6,7},{7,0},{8,9},{9,10},{10,1... | collective-permute-start | bytes 78344 | tf_op jit(solution)/shard_map/ppermute | solution.py:16
  13.4 6.8 %collective-permute-start.3 = (f32[1,3,16,68,2]{3,2,4,1,0:T(8,128)S(1)}, f32[1,3,16,68,2]{3,2,4,1,0:T(8,128)S(1)}, u32[]{:S(2)}, u32[]{:S(2)}) collective-permute-start(f32[1,3,16,68,2]{3,2,4,1,0:T(8,128)S(1)} %copy.114), channel_id=1, source_target_pairs={{1,0},{2,1},{3,2},{4,3},{5,4},{6,5},{7,6},{0,7},{9,8},{10,9},{11,1... | collective-permute-start | bytes 78344 | tf_op jit(solution)/shard_map/ppermute | solution.py:17
  156.2 3.3 %copy-start.10 = (f32[2,3,16,32,1]{4,3,2,1,0:T(8,128)S(1)}, f32[2,3,16,32,1]{4,3,2,1,0:T(8,128)}, u32[]{:S(2)}) copy-start(f32[2,3,16,32,1]{4,3,2,1,0:T(8,128)} %fusion.17) | copy-start | bytes 36868
  161.9 4.0 %copy-start.20 = (s32[2,7,2,4]{1,3,2,0:T(4,128)S(1)}, s32[2,7,2,4]{1,3,2,0:T(4,128)}, u32[]{:S(2)}) copy-start(s32[2,7,2,4]{1,3,2,0:T(4,128)} %param.3) | copy-start | bytes 1348
  162.9 6.6 %copy-start.8 = (f32[4,3,8,32,64]{4,3,2,1,0:T(8,128)}, f32[4,3,8,32,64]{4,3,2,1,0:T(8,128)S(1)}, u32[]{:S(2)}) copy-start(f32[4,3,8,32,64]{4,3,2,1,0:T(8,128)S(1)} %fusion.30) | copy-start | bytes 2359300
  162.9 4.8 %collective-permute-start.4 = (f32[1,3,8,2,64]{4,3,2,1,0:T(2,128)S(1)}, f32[1,3,8,2,64]{4,3,2,1,0:T(2,128)S(1)}, u32[]{:S(2)}, u32[]{:S(2)}) collective-permute-start(f32[1,3,8,2,64]{4,3,2,1,0:T(2,128)S(1)} %get-tuple-element.32), channel_id=1, source_target_pairs={{0,8},{8,16},{16,24},{24,0},{1,9},{9,17},{17,25},{25,1},{2,10},{10... | collective-permute-start | bytes 36872 | tf_op jit(solution)/shard_map/ppermute | solution.py:16
  165.4 3.8 %collective-permute-start.5 = (f32[1,3,8,2,64]{4,3,2,1,0:T(2,128)S(1)}, f32[1,3,8,2,64]{4,3,2,1,0:T(2,128)S(1)}, u32[]{:S(2)}, u32[]{:S(2)}) collective-permute-start(f32[1,3,8,2,64]{4,3,2,1,0:T(2,128)S(1)} %get-tuple-element.33), channel_id=1, source_target_pairs={{8,0},{16,8},{24,16},{0,24},{9,1},{17,9},{25,17},{1,25},{10,2},{18... | collective-permute-start | bytes 36872 | tf_op jit(solution)/shard_map/ppermute | solution.py:17
  169.5 15.1 %collective-permute-start.6 = (f32[1,3,8,36,2]{4,3,2,1,0:T(8,128)S(1)}, f32[1,3,8,36,2]{4,3,2,1,0:T(8,128)S(1)}, u32[]{:S(2)}, u32[]{:S(2)}) collective-permute-start(f32[1,3,8,36,2]{4,3,2,1,0:T(8,128)S(1)} %get-tuple-element.56), channel_id=1, source_target_pairs={{0,1},{1,2},{2,3},{3,4},{4,5},{5,6},{6,7},{7,0},{8,9},{9,10},{10,1... | collective-permute-start | bytes 20744 | tf_op jit(solution)/shard_map/ppermute | solution.py:16
  169.6 15.0 %collective-permute-start.7 = (f32[1,3,8,36,2]{4,3,2,1,0:T(8,128)S(1)}, f32[1,3,8,36,2]{4,3,2,1,0:T(8,128)S(1)}, u32[]{:S(2)}, u32[]{:S(2)}) collective-permute-start(f32[1,3,8,36,2]{4,3,2,1,0:T(8,128)S(1)} %get-tuple-element.57), channel_id=1, source_target_pairs={{1,0},{2,1},{3,2},{4,3},{5,4},{6,5},{7,6},{0,7},{9,8},{10,9},{11,1... | collective-permute-start | bytes 20744 | tf_op jit(solution)/shard_map/ppermute | solution.py:17
  199.1 3.3 copy-start.3
  199.2 3.2 copy-start.9
  199.4 5.0 %collective-permute-start.8 = (f32[4,3,8,1,32]{4,3,2,1,0:T(1,128)S(1)}, f32[4,3,8,1,32]{4,3,2,1,0:T(1,128)S(1)}, u32[]{:S(2)}, u32[]{:S(2)}) collective-permute-start(f32[4,3,8,1,32]{4,3,2,1,0:T(1,128)S(1)} %get-tuple-element.42), channel_id=1, source_target_pairs={{0,8},{8,16},{16,24},{24,0},{1,9},{9,17},{17,25},{25,1},{2,10},{10... | collective-permute-start | bytes 36872 | tf_op jit(solution)/shard_map/ppermute | solution.py:16
  201.0 4.1 %collective-permute-start.9 = (f32[4,3,8,1,32]{4,3,2,1,0:T(1,128)S(1)}, f32[4,3,8,1,32]{4,3,2,1,0:T(1,128)S(1)}, u32[]{:S(2)}, u32[]{:S(2)}) collective-permute-start(f32[4,3,8,1,32]{4,3,2,1,0:T(1,128)S(1)} %get-tuple-element.43), channel_id=1, source_target_pairs={{8,0},{16,8},{24,16},{0,24},{9,1},{17,9},{25,17},{1,25},{10,2},{18... | collective-permute-start | bytes 36872 | tf_op jit(solution)/shard_map/ppermute | solution.py:17
  209.7 5.5 %collective-permute-start.10 = (f32[4,3,8,18,1]{3,2,4,1,0:T(8,128)}, f32[4,3,8,18,1]{3,2,4,1,0:T(8,128)}, u32[]{:S(2)}, u32[]{:S(2)}) collective-permute-start(f32[4,3,8,18,1]{3,2,4,1,0:T(8,128)} %copy.120), channel_id=1, source_target_pairs={{1,0},{2,1},{3,2},{4,3},{5,4},{6,5},{7,6},{0,7},{9,8},{10,9},{11,1... | collective-permute-start | bytes 20744 | tf_op jit(solution)/shard_map/ppermute | solution.py:17
  214.7 5.7 %collective-permute-start.11 = (f32[4,3,8,18,1]{3,2,4,1,0:T(8,128)}, f32[4,3,8,18,1]{3,2,4,1,0:T(8,128)}, u32[]{:S(2)}, u32[]{:S(2)}) collective-permute-start(f32[4,3,8,18,1]{3,2,4,1,0:T(8,128)} %copy.122), channel_id=1, source_target_pairs={{0,1},{1,2},{2,3},{3,4},{4,5},{5,6},{6,7},{7,0},{8,9},{9,10},{10,1... | collective-permute-start | bytes 20744 | tf_op jit(solution)/shard_map/ppermute | solution.py:16
  237.6 4.1 %copy-start.12 = (f32[1,3,4,16,32]{3,2,1,0,4:T(4,128)S(1)}, f32[1,3,4,16,32]{3,2,1,0,4:T(4,128)}, u32[]{:S(2)}) copy-start(f32[1,3,4,16,32]{3,2,1,0,4:T(4,128)} %copy.141) | copy-start | bytes 73732
  238.7 23.1 %collective-permute-start.12 = (f32[4,3,16,1,64]{4,3,2,1,0:T(1,128)}, f32[4,3,16,1,64]{4,3,2,1,0:T(1,128)S(1)}, u32[]{:S(2)}, u32[]{:S(2)}) collective-permute-start(f32[4,3,16,1,64]{4,3,2,1,0:T(1,128)} %get-tuple-element.16), channel_id=1, source_target_pairs={{0,8},{8,16},{16,24},{24,0},{1,9},{9,17},{17,25},{25,1},{2,10},{10... | collective-permute-start | bytes 147464 | tf_op jit(solution)/shard_map/ppermute | solution.py:16
  239.7 22.1 %collective-permute-start.13 = (f32[4,3,16,1,64]{4,3,2,1,0:T(1,128)}, f32[4,3,16,1,64]{4,3,2,1,0:T(1,128)S(1)}, u32[]{:S(2)}, u32[]{:S(2)}) collective-permute-start(f32[4,3,16,1,64]{4,3,2,1,0:T(1,128)} %get-tuple-element.17), channel_id=1, source_target_pairs={{8,0},{16,8},{24,16},{0,24},{9,1},{17,9},{25,17},{1,25},{10,2},{18... | collective-permute-start | bytes 147464 | tf_op jit(solution)/shard_map/ppermute | solution.py:17
  262.6 4.5 %copy-start = (f32[4,3,16,34,64]{4,3,2,1,0:T(8,128)}, f32[4,3,16,34,64]{4,3,2,1,0:T(8,128)S(1)}, u32[]{:S(2)}) copy-start(f32[4,3,16,34,64]{4,3,2,1,0:T(8,128)S(1)} %pad_maximum_fusion.3) | copy-start | bytes 5013508
  270.7 17.0 %collective-permute-start.14 = (f32[4,3,16,34,1]{3,2,4,1,0:T(8,128)}, f32[4,3,16,34,1]{3,2,4,1,0:T(8,128)}, u32[]{:S(2)}, u32[]{:S(2)}) collective-permute-start(f32[4,3,16,34,1]{3,2,4,1,0:T(8,128)} %copy.132), channel_id=1, source_target_pairs={{1,0},{2,1},{3,2},{4,3},{5,4},{6,5},{7,6},{0,7},{9,8},{10,9},{11,1... | collective-permute-start | bytes 78344 | tf_op jit(solution)/shard_map/ppermute | solution.py:17
  287.7 9.0 %collective-permute-start.15 = (f32[4,3,16,34,1]{3,2,4,1,0:T(8,128)S(1)}, f32[4,3,16,34,1]{3,2,4,1,0:T(8,128)S(1)}, u32[]{:S(2)}, u32[]{:S(2)}) collective-permute-start(f32[4,3,16,34,1]{3,2,4,1,0:T(8,128)S(1)} %copy.134), channel_id=1, source_target_pairs={{0,1},{1,2},{2,3},{3,4},{4,5},{5,6},{6,7},{7,0},{8,9},{9,10},{10,1... | collective-permute-start | bytes 78344 | tf_op jit(solution)/shard_map/ppermute | solution.py:16
  299.7 3.9 %copy-start.1 = (f32[4,3,16,34,64]{4,3,2,1,0:T(8,128)S(1)}, f32[4,3,16,34,64]{4,3,2,1,0:T(8,128)}, u32[]{:S(2)}) copy-start(f32[4,3,16,34,64]{4,3,2,1,0:T(8,128)} %copy-done) | copy-start | bytes 5013508
  (13 other events, 23.2 us)
where the time goes:
time: 332 us; the launch traced here: 327 us
  local copies, waits for them, and re-layouts  202 us (61%)
  other arithmetic  51.8 us (16%)
  blocking collectives  29.7 us (9%)
  starting transfers between devices  22.1 us (7%)
  waiting for transfers between devices  19.9 us (6%)
    slice x16, local copies, waits for them, and re-layouts, take_slice(): return lax.slice_in_dim(volume, start, stop, stride, direction)  137 us
    all_gather x1, blocking collectives, gather_coarse(): partial_rows = lax.all_gather(local_coarse, 'gy', axis=3, tiled=True)  18.4 us
    ppermute x8, waiting for transfers between devices, extended(): before = lax.ppermute(last, axis, up)  16.8 us
    slice x11, local copies, waits for them, and re-layouts, extended(): last = lax.slice_in_dim(x, length - width, length, axis=dim)  15.8 us
    concatenate x8, other arithmetic, extended(): x = jnp.concatenate([before, x, after], axis=dim)  15.1 us
    ppermute x8, starting transfers between devices, extended(): after = lax.ppermute(leading, axis, down)  13.5 us
    sub x6, other arithmetic, lift_inverse(): take_slice(smooth_pad, 1, length + 2, 1, direction)  11.4 us
    all_gather x1, blocking collectives, gather_coarse(): return lax.all_gather(partial_rows, 'gx', axis=2, tiled=True)  11.4 us
  transfers between devices with their start and end apart: 16, of which 8 were waited for; matrix products, arithmetic and copies ran while one was open for 9% of the time, Pallas kernels for 0%

commit v1 on v0

v1 whole, which is shorter than its diff:
```python
import functools

import jax
import jax.numpy as jnp
import ml_dtypes
import numpy as np
from jax import lax
from jax.experimental import pallas as pl
from jax.experimental.pallas import tpu as pltpu
from jax.sharding import PartitionSpec as P

F32 = jnp.float32
BF16 = jnp.bfloat16
VMEM_LIMIT = 48 * 1024 * 1024

NV, NZ, NR, NL = 3, 16, 64, 128
HALO = 8


def detail_row(k):
    return {2 * k + 1: 1.0, 2 * k: -0.5, 2 * k + 2: -0.5}


def smooth_row(k):
    row = {2 * k: 1.0}
    for j in (k - 1, k):
        for cell, value in detail_row(j).items():
            row[cell] = row.get(cell, 0.0) + 0.25 * value
    return row


def even_row(k):
    return {("s", k): 1.0, ("d", k - 1): -0.25, ("d", k): -0.25}


def odd_row(k):
    row = {("d", k): 1.0}
    for j in (k, k + 1):
        for name, value in even_row(j).items():
            row[name] = row.get(name, 0.0) + 0.5 * value
    return row


def as_bf16(matrix):
    cast = matrix.astype(ml_dtypes.bfloat16)
    assert (cast.astype(np.float64) == matrix).all()
    return cast


def cell_place(y):
    return y if 0 <= y < NL else (y + HALO + NL if y < 0 else y + HALO)


def fill_forward(matrix, place_in, column, row):
    for cell, value in row.items():
        matrix[place_in(cell), column] += value


def level_one_columns():
    names = {("s", k): k for k in range(65)}
    names.update({("d", k): 128 + k for k in range(65)})
    names[("d", -1)] = 128 + 65
    return names


def level_two_columns():
    names = {("s", k): k for k in range(33)}
    names.update({("d", k): 64 + k for k in range(33)})
    names[("d", -1)] = 64 + 33
    return names


def smooth_place(k):
    return k + 2


@functools.lru_cache(maxsize=None)
def weights():
    w = {}
    names = level_one_columns()
    forward = np.zeros((144, 256))
    inverse = np.zeros((256, 128))
    for (kind, k), column in names.items():
        fill_forward(forward, cell_place, column, smooth_row(k) if kind == "s" else detail_row(k))
    for k in range(64):
        for y, row in ((2 * k, even_row(k)), (2 * k + 1, odd_row(k))):
            for name, value in row.items():
                inverse[names[name], y] += value
    w["forward"], w["inverse"] = forward, inverse
    smooth = np.zeros((256, 128))
    for k in range(-2, 67):
        fill_forward(smooth, cell_place, smooth_place(k), smooth_row(k))
    w["smooth"] = smooth
    names2 = level_two_columns()
    forward2 = np.zeros((128, 128))
    inverse2 = np.zeros((128, 128))
    for (kind, k), column in names2.items():
        fill_forward(forward2, smooth_place, column, smooth_row(k) if kind == "s" else detail_row(k))
    for k in range(33):
        rows = [(2 * k, even_row(k))] + ([(2 * k + 1, odd_row(k))] if k < 32 else [])
        for y, row in rows:
            for name, value in row.items():
                inverse2[names2[name], y] += value
    w["forward2"], w["inverse2"] = forward2, inverse2
    back = np.zeros((256, 128))
    back[:65] = inverse[:65]
    back[128 : 128 + 65] = inverse[:65]
    w["back"] = back
    plane = np.zeros((2, 8, NZ))

    def mirrored(z):
        return -z if z < 0 else (2 * (NZ - 1) - z if z > NZ - 1 else z)

    for k in range(8):
        for z, value in smooth_row(k).items():
            plane[0, k, mirrored(z)] += value
        for z, value in detail_row(k).items():
            plane[1, k, mirrored(z)] += value
    halo = np.zeros((4, 128, 2, 8, 16))
    for bz in range(2):
        for k in range(8):
            for z in range(NZ):
                for c in range(HALO):
                    left = 8 * ((z - 1) % NZ) + c
                    right = 8 * z + c
                    halo[0:2, left, bz, k, c] = plane[bz, k, z]
                    halo[2:4, right, bz, k, 8 + c] = plane[bz, k, z]
    w["halo"] = halo.reshape(512, 256)
    spread = np.zeros((3, 128, 2, 128))
    for k in range(64):
        spread[0, k, 0, k] = 1
    spread[1, 0, 0, 64] = 1
    spread[2, 63, 0, 65] = 1
    for k in range(32):
        spread[0, 64 + k, 1, k] = 1
        spread[0, 64 + k, 1, 64 + k] = 1
    for base in (0, 64):
        spread[1, 64, 1, base + 32] = 1
        spread[2, 95, 1, base + 33] = 1
    w["spread"] = spread.reshape(384, 256)
    expand = np.zeros((2, 4, 128))
    for j in range(4):
        expand[0, j, 16 * j : 16 * j + 16] = 1
        expand[1, j, 64 + 8 * j : 64 + 8 * j + 8] = 1
    w["expand"] = expand
    twice = {}
    for k, value in smooth_row(0).items():
        for y, other in smooth_row(k).items():
            twice[y] = twice.get(y, 0.0) + value * other
    columns = np.zeros((NV, 2, 128, 128))
    for m in range(-1, 34):
        for t, value in twice.items():
            if 0 <= 4 * m + t < NL:
                for v in range(NV):
                    columns[v, :, 4 * m + t, 40 * v + m + 1] = value
    w["part_columns"] = columns.reshape(NV * 256, 128)
    rows = np.zeros((24, 2, 64))
    for m in range(-1, 18):
        for t, value in twice.items():
            if 0 <= 4 * m + t < NR:
                rows[m % 24, :, 4 * m + t] = value
    w["part_rows"] = rows.reshape(24, 128)
    return {name: as_bf16(matrix) for name, matrix in w.items()}


def two_terms(x):
    high = x.astype(BF16)
    low = (x - high.astype(F32)).astype(BF16)
    return high, low


def dot(a, b):
    return jnp.dot(a, b, preferred_element_type=F32)


def lift_planes(cells):
    half = len(cells) // 2
    even, odd = cells[0::2], cells[1::2]
    detail = [odd[k] - 0.5 * (even[k] + even[min(k + 1, half - 1)]) for k in range(half)]
    smooth = [even[k] + 0.25 * (detail[max(k - 1, 0)] + detail[k]) for k in range(half)]
    return smooth, detail


def unlift_planes(smooth, detail):
    half = len(smooth)
    even = [smooth[k] - 0.25 * (detail[max(k - 1, 0)] + detail[k]) for k in range(half)]
    out = []
    for k in range(half):
        out += [even[k], detail[k] + 0.5 * (even[k] + even[min(k + 1, half - 1)])]
    return out


def lift_rows(load, start):
    even, odd, after = load(start), load(start + 1), load(start + 2)
    before, odd_before = load(start - 2), load(start - 1)
    detail = odd - 0.5 * (even + after)
    detail_before = odd_before - 0.5 * (before + even)
    return even + 0.25 * (detail_before + detail), detail


def unlift_rows(smooth, detail, row):
    here, after = detail(row), detail(row + 1)
    even = smooth(row) - 0.25 * (detail(row - 1) + here)
    next_even = smooth(row + 1) - 0.25 * (here + after)
    return even, here + 0.5 * (even + next_even)


def pack_kernel(field, masks, expand, part_columns, part_rows, top, bottom, left, right, own_masks, share, wide):
    lane = lax.broadcasted_iota(jnp.int32, (8, NL), 1) // 8

    def pack_rows(step, _):
        v, t = step // 8, step % 8
        rows = pl.ds(pl.multiple_of(t * 8, 8), 8)
        low = jnp.zeros((8, NL), F32)
        high = jnp.zeros((8, NL), F32)
        for z in range(NZ):
            x = field[v, z, rows, :]
            turned = pltpu.roll(x, 8 * z, 1) if z else x
            low = jnp.where(lane == z, turned, low)
            high = jnp.where(lane == (z - 1) % NZ, turned, high)
        left[v, rows, :] = low
        right[v, rows, :] = high
        return 0

    lax.fori_loop(0, NV * 8, pack_rows, 0)
    for v in range(NV):
        top[v] = left[v, 0:8, :]
        top[3 + v] = right[v, 0:8, :]
        bottom[v] = left[v, NR - 8 : NR, :]
        bottom[3 + v] = right[v, NR - 8 : NR, :]
        top[8 + v * NZ : 8 + (v + 1) * NZ] = field[v, :, 0:8, :]
        bottom[8 + v * NZ : 8 + (v + 1) * NZ] = field[v, :, NR - 8 : NR, :]
    for i, out in ((0, top), (1, bottom)):
        tile = jnp.zeros((7, NL), F32)
        for l in range(2):
            flags = masks[l, i].astype(F32).astype(BF16)
            tile += lax.dot_general(flags, expand[l], (((0,), (0,)), ((), ())), preferred_element_type=F32)
        own_masks[i] = jnp.concatenate([tile, jnp.zeros((1, NL), F32)], 0)
        out[6] = own_masks[i]
        out[7] = jnp.zeros((8, NL), F32)

    def columns(step, _):
        planes = pl.ds(step * 4, 4)
        terms = []
        for v in range(NV):
            terms += list(two_terms(field[v, planes].reshape(4 * NR, NL)))
        wide[planes] = dot(jnp.concatenate(terms, 1), part_columns[...]).reshape(4, NR, NL)
        return 0

    lax.fori_loop(0, NZ // 4, columns, 0)
    smooth, _ = lift_planes([wide[z] for z in range(NZ)])
    smooth, _ = lift_planes(smooth)
    high, low = two_terms(jnp.concatenate(smooth, 1))
    part = dot(part_rows[...], jnp.concatenate([high, low], 0))
    for z in range(4):
        share[z * 24 : (z + 1) * 24, :] = part[:, z * NL : (z + 1) * NL]


def pack(field, masks):
    w = weights()
    shapes = [(56, 8, NL), (56, 8, NL), (NV, NR, NL), (NV, NR, NL), (2, 8, NL), (96, NL)]
    vmem = pl.BlockSpec(memory_space=pltpu.VMEM)
    return pl.pallas_call(
        pack_kernel,
        out_shape=[jax.ShapeDtypeStruct(s, F32) for s in shapes],
        in_specs=[vmem] * 5,
        out_specs=[vmem] * 6,
        scratch_shapes=[pltpu.VMEM((NZ, NR, NL), F32)],
        compiler_params=pltpu.CompilerParams(vmem_limit_bytes=VMEM_LIMIT),
    )(field, masks.transpose(0, 2, 3, 1), w["expand"], w["part_columns"], w["part_rows"])


def join_kernel(left, right, own_masks, north, south, to_left, to_right):
    for v in range(NV):
        for side, tile, out in ((left, v, to_left), (right, 3 + v, to_right)):
            out[v * 80 : v * 80 + 64, :] = side[v]
            out[v * 80 + 64 : v * 80 + 72, :] = south[tile]
            out[v * 80 + 72 : v * 80 + 80, :] = north[tile]
    for out in (to_left, to_right):
        out[240:248, :] = north[6]
        out[248:256, :] = own_masks[0]
        out[256:264, :] = own_masks[1]
        out[264:272, :] = south[6]


def join(left, right, own_masks, north, south):
    whole = pl.BlockSpec((NV, NR, NL), lambda i: (0, 0, 0))
    edge = pl.BlockSpec((8, 8, NL), lambda i: (0, 0, 0))
    out = pl.BlockSpec((272, NL), lambda i: (0, 0))
    return pl.pallas_call(
        join_kernel,
        grid=(1,),
        out_shape=[jax.ShapeDtypeStruct((272, NL), F32)] * 2,
        in_specs=[whole, whole, pl.BlockSpec((2, 8, NL), lambda i: (0, 0, 0)), edge, edge],
        out_specs=[out, out],
        compiler_params=pltpu.CompilerParams(vmem_limit_bytes=VMEM_LIMIT),
    )(left, right, own_masks, north, south)


def wave_kernel(
    field, north, south, west, east, own_masks,
    forward, inverse, smooth_w, forward2, inverse2, back, halo_w, spread,
    out,
    cells, first, halo_x, halo, gain, gain2, low, second, kept2, low_back, kept, sems,
):
    copies = []
    for v in range(NV):
        planes = pl.ds(8 + v * NZ, NZ)
        pairs = [
            (field.at[v], cells.at[v, 0:NZ, 8:72, :]),
            (north.at[planes], cells.at[v, 0:NZ, 0:8, :]),
            (north.at[planes], cells.at[v, 0:NZ, 80:88, :]),
            (south.at[planes], cells.at[v, 0:NZ, 72:80, :]),
            (field.at[v, :, 0:8, :], cells.at[v, 0:NZ, 88:96, :]),
        ]
        for p, ref in ((NZ, west), (NZ + 1, east)):
            pairs += [
                (ref.at[v * 80 : v * 80 + 80, :], cells.at[v, p, 8:88, :]),
                (ref.at[v * 80 + 72 : v * 80 + 80, :], cells.at[v, p, 0:8, :]),
                (ref.at[v * 80 : v * 80 + 8, :], cells.at[v, p, 88:96, :]),
            ]
        copies.append([
            pltpu.make_async_copy(source, target, sems.at[v, n]) for n, (source, target) in enumerate(pairs)
        ])
        for copy in copies[-1]:
            copy.start()
    tiles = [pltpu.make_async_copy(ref.at[240:272, :], cells.at[0, 18 + n, 0:32, :], sems.at[3, n])
             for n, ref in enumerate((west, east))]
    tiles += [pltpu.make_async_copy(north.at[6], cells.at[0, 20, 0:8, :], sems.at[3, 2]),
              pltpu.make_async_copy(south.at[6], cells.at[0, 20, 24:32, :], sems.at[3, 3])]
    for copy in tiles:
        copy.start()
    for copy in tiles:
        copy.wait()

    own = jnp.concatenate([cells[0, 20, 0:8, :], own_masks[0], own_masks[1], cells[0, 20, 24:32, :]], 0)
    flags = jnp.concatenate([own, cells[0, 19, 0:32, :], cells[0, 18, 0:32, :]], 1).astype(BF16)
    lanes = dot(flags, spread[...])
    lane64 = lax.broadcasted_iota(jnp.int32, (1, NL), 1) < 64
    zero, one = jnp.zeros((1, NL), F32), jnp.ones((1, NL), F32)
    forward_f, forward2_f = forward[...].astype(F32), forward2[...].astype(F32)
    for ib in range(4):
        for bz in range(2):
            for bx in range(2):
                n = 2 * bz + bx
                b = 8 * ib + 4 * bz + bx - 1
                smooth_one = lanes[b : b + 1, 0:NL] if n else zero
                detail_one = lanes[b + 2 : b + 3, 0:NL]
                row = jnp.concatenate([smooth_one, detail_one], 1)
                gain[ib, n, 0:144, :] = dot((forward_f * row).astype(BF16), inverse[...]).astype(BF16)
                gain[ib, n, 144:256, :] = jnp.zeros((112, NL), BF16)
                smooth_two = lanes[b : b + 1, NL:] if n else one
                row = jnp.where(lane64, smooth_two, lanes[b + 2 : b + 3, NL:])
                both = dot((forward2_f * row).astype(BF16), inverse2[...]).astype(BF16)
                gain2[ib, n, 0:128, :] = both
                gain2[ib, n, 128:256, :] = both

    for v in range(NV):
        for copy in copies[v]:
            copy.wait()

        def rows_one(t, _):
            at = pl.multiple_of(t * 8, 8)
            lifted = [
                lift_rows(lambda s: cells[v, p, pl.ds(16 * t + s, 8, stride=2), :], 8) for p in range(NZ + 2)
            ]
            for bx in range(2):
                smooth, detail = lift_planes([pair[bx] for pair in lifted[:NZ]])
                for bz, part in ((0, smooth), (1, detail)):
                    for z in range(8):
                        first[2 * bz + bx, v * 8 + z, pl.ds(at, 8), :] = part[z]
                halo_x[bx, v, pl.ds(at, 8), 0:NL] = lifted[NZ][bx]
                halo_x[bx, v, pl.ds(at, 8), NL:] = lifted[NZ + 1][bx]
            return 0

        lax.fori_loop(0, 5, rows_one, 0)
    for bx in range(2):
        high, low_term = two_terms(halo_x[bx].reshape(NV * 40, 256))
        terms = jnp.concatenate([high[:, :NL], low_term[:, :NL], high[:, NL:], low_term[:, NL:]], 1)
        halo[bx] = dot(terms, halo_w[...]).reshape(NV, 40, 256)

    def operand(n, v, at, count):
        bz, bx = n // 2, n % 2
        rows = pl.ds(at, count)
        main = first[n, pl.ds(v * 8, 8), rows, :].reshape(8 * count, NL)
        beside = halo[bx, v, rows, bz * NL : (bz + 1) * NL]
        sides = jnp.concatenate([pltpu.roll(beside, (NL - 16 * z) % NL, 1) if z else beside for z in range(8)], 0)
        return two_terms(jnp.concatenate([main, sides], 1))

    def smooth_part(v, _):
        planes = pl.ds(v * 8, 8)
        for at, count in ((0, 16), (16, 16), (32, 8)):
            high, low_term = operand(0, v, at, count)
            part = (dot(high, smooth_w[...]) + dot(low_term, smooth_w[...])).reshape(8, count, NL)
            if at < 32:
                low[planes, 8 + at : 8 + at + count, :] = part
                if at == 0:
                    low[planes, 56:64, :] = part[:, 0:8]
            else:
                low[planes, 0:8, :] = part
                low[planes, 40:48, :] = part
                low[planes, 48:56, :] = part
        return 0

    lax.fori_loop(0, NV, smooth_part, 0)

    def rows_two(v, _):
        for t in range(3):
            lifted = [
                lift_rows(lambda s: low[v * 8 + p, pl.ds(16 * t + s, 8, stride=2), :], 8) for p in range(8)
            ]
            for bx in range(2):
                smooth, detail = lift_planes([pair[bx] for pair in lifted])
                for bz, part in ((0, smooth), (1, detail)):
                    for z in range(4):
                        second[2 * bz + bx, t, pl.ds(pl.multiple_of((v * 4 + z) * 8, 8), 8), :] = part[z]
        return 0

    lax.fori_loop(0, NV, rows_two, 0)
    ext_two = lax.broadcasted_iota(jnp.int32, (NV * 4, 8, NL), 1) < 4
    for n in range(4):
        for t in range(3):
            terms = jnp.concatenate(two_terms(second[n, t]), 1)
            if t < 2:
                kept2[n, :, 8 + 8 * t : 16 + 8 * t, :] = dot(terms, gain2[t + 1, n]).reshape(NV * 4, 8, NL)
            else:
                below = dot(terms, gain2[3, n]).reshape(NV * 4, 8, NL)
                above = dot(terms, gain2[0, n]).reshape(NV * 4, 8, NL)
                part = jnp.where(ext_two, below, above)
                kept2[n, :, 0:8, :] = part
                kept2[n, :, 24:32, :] = part

    def back_two(v, _):
        for t in range(3):
            pairs = {}
            for bz in range(2):
                for z in range(4):
                    p = v * 4 + z
                    if t < 2:
                        pairs[bz, z] = unlift_rows(
                            lambda r: kept2[2 * bz, p, pl.ds(r, 8), :],
                            lambda r: kept2[2 * bz + 1, p, pl.ds(r, 8), :],
                            8 + 8 * t,
                        )
                    else:
                        even = kept2[2 * bz, p, 24:32, :] - 0.25 * (
                            kept2[2 * bz + 1, p, 23:31, :] + kept2[2 * bz + 1, p, 24:32, :]
                        )
                        pairs[bz, z] = (even, even)
            for parity in range(2 if t < 2 else 1):
                planes = unlift_planes([pairs[0, z][parity] for z in range(4)], [pairs[1, z][parity] for z in range(4)])
                for z in range(8):
                    low_back[v * 8 + z, pl.ds(16 * t + parity, 8, stride=2), :] = planes[z]
        return 0

    lax.fori_loop(0, NV, back_two, 0)

    ext_one = lax.broadcasted_iota(jnp.int32, (8, 8, NL), 1) < 4

    def keep(v, _):
        planes = pl.ds(v * 8, 8)
        for n in range(4):
            for ib in range(3):
                at, count = 16 * ib, 16 if ib < 2 else 8
                high, low_term = operand(n, v, at, count)
                if n == 0:
                    terms = jnp.concatenate(two_terms(low_back[planes, at : at + count, :].reshape(8 * count, NL)), 1)
                    base = dot(terms, back[...])
                if ib < 2:
                    part = dot(high, gain[ib + 1, n]) + dot(low_term, gain[ib + 1, n])
                    if n == 0:
                        part = part + base
                    kept[n, planes, 8 + at : 24 + at, :] = part.reshape(8, count, NL)
                else:
                    below = dot(high, gain[3, n]) + dot(low_term, gain[3, n])
                    above = dot(high, gain[0, n]) + dot(low_term, gain[0, n])
                    if n == 0:
                        below = below + base
                    part = jnp.where(ext_one, below.reshape(8, 8, NL), above.reshape(8, 8, NL))
                    kept[n, planes, 0:8, :] = part
                    kept[n, planes, 40:48, :] = part
        return 0

    lax.fori_loop(0, NV, keep, 0)

    def back_one(step, _):
        v, t = step // 4, step % 4
        pairs = {}
        for bz in range(2):
            for z in range(8):
                p = v * 8 + z
                pairs[bz, z] = unlift_rows(
                    lambda r: kept[2 * bz, p, pl.ds(8 * t + r, 8), :],
                    lambda r: kept[2 * bz + 1, p, pl.ds(8 * t + r, 8), :],
                    8,
                )
        for parity in range(2):
            planes = unlift_planes([pairs[0, z][parity] for z in range(8)], [pairs[1, z][parity] for z in range(8)])
            for z in range(NZ):
                out[v, z, pl.ds(16 * t + parity, 8, stride=2), :] = planes[z]
        return 0

    lax.fori_loop(0, NV * 4, back_one, 0)


def wave(field, north, south, west, east, own_masks):
    w = weights()
    vmem = pl.BlockSpec(memory_space=pltpu.VMEM)
    anywhere = pl.BlockSpec(memory_space=pl.ANY)
    names = ["forward", "inverse", "smooth", "forward2", "inverse2", "back", "halo", "spread"]
    return pl.pallas_call(
        wave_kernel,
        out_shape=jax.ShapeDtypeStruct((NV, NZ, NR, NL), F32),
        in_specs=[anywhere] * 5 + [vmem] * (1 + len(names)),
        out_specs=vmem,
        scratch_shapes=[
            pltpu.VMEM((NV, 21, 96, NL), F32),
            pltpu.VMEM((4, NV * 8, 40, NL), F32),
            pltpu.VMEM((2, NV, 40, 256), F32),
            pltpu.VMEM((2, NV, 40, 256), F32),
            pltpu.VMEM((4, 4, 256, NL), BF16),
            pltpu.VMEM((4, 4, 256, NL), BF16),
            pltpu.VMEM((NV * 8, 64, NL), F32),
            pltpu.VMEM((4, 3, NV * 32, NL), F32),
            pltpu.VMEM((4, NV * 4, 40, NL), F32),
            pltpu.VMEM((NV * 8, 48, NL), F32),
            pltpu.VMEM((4, NV * 8, 48, NL), F32),
            pltpu.SemaphoreType.DMA((4, 11)),
        ],
        compiler_params=pltpu.CompilerParams(vmem_limit_bytes=VMEM_LIMIT),
    )(field, north, south, west, east, own_masks, *[w[name] for name in names])


def coarse_kernel(count_x, count_y, shares, out):
    lane = lax.broadcasted_iota(jnp.int32, (16, NL), 1)
    row = lax.broadcasted_iota(jnp.int32, (8, NL), 0)

    def block(i, _):
        before, after = lax.rem(i + count_x - 1, count_x), lax.rem(i + 1, count_x)
        for z in range(4):
            pieces = []
            for j in range(count_y):
                first = shares[i, j, 24 * z : 24 * z + 8, :]
                second = shares[i, j, 24 * z + 8 : 24 * z + 16, :]
                first += jnp.where(row < 4, shares[before, j, 24 * z + 16 : 24 * z + 24, :], 0.0)
                second += jnp.where(row < 4, 0.0, shares[after, j, 24 * z + 16 : 24 * z + 24, :])
                pieces.append(jnp.concatenate([first, second], 0))
            for v in range(NV):
                for t in range(count_y // 4):
                    total = jnp.zeros((16, NL), F32)
                    for q in range(-1, 5):
                        start = 32 * q - 1
                        turned = pltpu.roll(pieces[(4 * t + q) % count_y], (start - 40 * v) % NL, 1)
                        total += jnp.where((lane >= start) & (lane < start + 35), turned, 0.0)
                    out[v, z, pl.ds(pl.multiple_of(16 * i, 16), 16), NL * t : NL * (t + 1)] = total
        return 0

    lax.fori_loop(0, count_x, block, 0)


def coarse_of(shares, count_x, count_y):
    vmem = pl.BlockSpec(memory_space=pltpu.VMEM)
    return pl.pallas_call(
        functools.partial(coarse_kernel, count_x, count_y),
        out_shape=jax.ShapeDtypeStruct((NV, 4, 16 * count_x, 32 * count_y), F32),
        in_specs=[vmem],
        out_specs=vmem,
        compiler_params=pltpu.CompilerParams(vmem_limit_bytes=VMEM_LIMIT),
    )(shares.reshape(count_x, count_y, 96, NL))


def shifts(axis):
    count = lax.axis_size(axis)
    up = [(i, (i + 1) % count) for i in range(count)]
    return up, [(j, i) for i, j in up]


def body(field, masks):
    count_x, count_y = lax.axis_size("gx"), lax.axis_size("gy")
    top, bottom, left, right, own_masks, share = pack(field, masks)
    shares = lax.all_gather(share, ("gx", "gy"), axis=0, tiled=True)
    up, down = shifts("gx")
    north = lax.ppermute(bottom, "gx", up)
    south = lax.ppermute(top, "gx", down)
    to_left, to_right = join(left, right, own_masks, north, south)
    up, down = shifts("gy")
    west = lax.ppermute(to_right, "gy", up)
    east = lax.ppermute(to_left, "gy", down)
    restored = wave(field, north, south, west, east, own_masks)
    return restored, coarse_of(shares, count_x, count_y)


def solution(mesh):
    placed = P(None, None, "gx", "gy")
    return jax.shard_map(
        body,
        mesh=mesh,
        in_specs=(placed, placed),
        out_specs=(placed, P()),
        check_vma=False,
    )
```

time: 332 us -> 85.7 us (0.26); the launches traced: 327 us -> 85.4 us
  local copies, waits for them, and re-layouts: 202 us -> 5.85 us
  other arithmetic: 51.8 us -> 0 us
  blocking collectives: 29.7 us -> 0 us
  waiting for transfers between devices: 19.9 us -> 43.5 us
  starting transfers between devices: 22.1 us -> 7.64 us
  Pallas kernels: 0 us -> 14.2 us
  between operations: 1.55 us -> 14.2 us
    slice x37 -> x0, local copies, waits for them, and re-layouts: 171 us -> none  [the longest x16 137 us: take_slice(): return lax.slice_in_dim(volume, start, stop, stride, direction)]
    all_gather x2 -> x0, blocking collectives: 29.7 us -> none  [the longest x1 18.4 us: gather_coarse(): partial_rows = lax.all_gather(local_coarse, 'gy', axis=3, tiled=True)]
    all_gather x0 -> x1, waiting for transfers between devices: none -> 29.4 us  [body(): shares = lax.all_gather(share, ('gx', 'gy'), axis=0, tiled=True)]
    sub x18 -> x0, other arithmetic: 20.7 us -> none  [the longest x6 11.4 us: lift_inverse(): take_slice(smooth_pad, 1, length + 2, 1, direction)]
    concatenate x14 -> x0, other arithmetic: 16.4 us -> none  [the longest x8 15.1 us: extended(): x = jnp.concatenate([before, x, after], axis=dim)]
    ppermute x6 -> x0, local copies, waits for them, and re-layouts: 15.4 us -> none  [the longest x3 8.14 us: extended(): after = lax.ppermute(leading, axis, down)]
    ppermute x16 -> x4, starting transfers between devices: 22.1 us -> 7.6 us  [the longest x1 3.53 us: body(): east = lax.ppermute(to_left, 'gy', down)]
    pallas_call x0 -> x4, Pallas kernels: none -> 14.2 us  [the longest x1 8.06 us: wave(): pl.pallas_call(wave_kernel, out_shape=jax.ShapeDtypeStruct((NV, NZ, NR, N...]
  transfers between devices with their start and end apart: 16 -> 5, of which waited for: 8 -> 4; matrix products, arithmetic and copies ran while one was open for 9% -> 0% of each run, Pallas kernels for 0% -> 9%
where the time goes in v1:
time: 85.7 us; the launch traced here: 85.4 us
  waiting for transfers between devices  43.5 us (51%)
  Pallas kernels  14.2 us (17%)
  between operations  14.2 us (17%)
  starting transfers between devices  7.64 us (9%)
  local copies, waits for them, and re-layouts  5.85 us (7%)
    all_gather x1, waiting for transfers between devices, body(): shares = lax.all_gather(share, ('gx', 'gy'), axis=0, tiled=True)  29.4 us
    pallas_call x1, Pallas kernels, wave(): pl.pallas_call(wave_kernel, out_shape=jax.ShapeDtypeStruct((NV, NZ, NR, N...  8.06 us
    ppermute x1, waiting for transfers between devices, body(): north = lax.ppermute(bottom, 'gx', up)  6.37 us
    unnamed x30, local copies, waits for them, and re-layouts  5.85 us
    ppermute x1, waiting for transfers between devices, body(): south = lax.ppermute(top, 'gx', down)  4.64 us
    pallas_call x1, Pallas kernels, pack(): pl.pallas_call(pack_kernel, out_shape=[jax.ShapeDtypeStruct(s, F32) for s...  4.14 us
    ppermute x1, starting transfers between devices, body(): east = lax.ppermute(to_left, 'gy', down)  3.53 us
    ppermute x1, waiting for transfers between devices, body(): west = lax.ppermute(to_right, 'gy', up)  3.06 us
  transfers between devices with their start and end apart: 5, of which 4 were waited for; matrix products, arithmetic and copies ran while one was open for 0% of the time, Pallas kernels for 9%

profile of v1, /device:TPU:0, one launch (start us, length us, event | category | flops | bytes accessed | tf_op | source)
XLA Modules:
  0.0 85.4 jit_solution(16163336524386079990)
XLA Ops:
  7.2 0.0 all-gather.2.cloned.1.call-start
  7.2 1.4 %copy-done = f32[3,16,64,128]{3,2,1,0:T(8,128)S(1)} copy-done((f32[3,16,64,128]{3,2,1,0:T(8,128)S(1)}, f32[3,16,64,128]{3,2,1,0:T(8,128)}, u32[]{:S(2)}) %copy-start) | copy-done | bytes 1572888
  8.6 0.9 %copy-done.5 = bf16[768,128]{1,0:T(8,128)(2,1)S(1)} copy-done((bf16[768,128]{1,0:T(8,128)(2,1)S(1)}, bf16[768,128]{1,0:T(8,128)(2,1)}, u32[]{:S(2)}) %copy-start.5) | copy-done | bytes 196632
  9.5 0.7 copy-done.12
  10.2 0.7 copy-done.13
  10.9 0.7 copy-done.14
  11.6 0.0 copy-start.7
  11.6 0.0 copy-start.8
  11.7 0.0 copy-start.9
  11.7 0.0 copy-start.10
  11.7 0.0 copy-start.11
  11.7 4.1 %shard_map.140 = (f32[56,8,128]{2,1,0:T(8,128)S(1)}, f32[56,8,128]{2,1,0:T(8,128)S(1)}, f32[3,64,128]{2,1,0:T(8,128)S(1)}, f32[3,64,128]{2,1,0:T(8,128)S(1)}, f3...) custom-call(f32[3,16,64,128]{3,2,1,0:T(8,128)S(1)} %copy-done, s32[2,2,4,7]{3,2,1,0:T(4,128)S(1)} %bitcast.3, ...), custom_call_target="tpu_custom_call" | custom-call | tf_op jit(solution)/shard_map/pallas_call | solution.py:263
  15.8 0.0 all-gather.2.cloned.1.call-update
  15.9 3.0 %collective-permute-start = (f32[56,8,128]{2,1,0:T(8,128)S(1)}, f32[56,8,128]{2,1,0:T(8,128)S(1)}, u32[]{:S(2)}, u32[]{:S(2)}) collective-permute-start(f32[56,8,128]{2,1,0:T(8,128)S(1)} %get-tuple-element.10), channel_id=1, source_target_pairs={{0,8},{8,16},{16,24},{24,0},{1,9},{9,17},{17,25},{25,1},{2,10},{10... | collective-permute-start | bytes 688136 | tf_op jit(solution)/shard_map/ppermute | solution.py:583
  18.8 1.0 %collective-permute-start.1 = (f32[56,8,128]{2,1,0:T(8,128)S(1)}, f32[56,8,128]{2,1,0:T(8,128)S(1)}, u32[]{:S(2)}, u32[]{:S(2)}) collective-permute-start(f32[56,8,128]{2,1,0:T(8,128)S(1)} %get-tuple-element.11), channel_id=1, source_target_pairs={{8,0},{16,8},{24,16},{0,24},{9,1},{17,9},{25,17},{1,25},{10,2},{18... | collective-permute-start | bytes 688136 | tf_op jit(solution)/shard_map/ppermute | solution.py:584
  19.9 6.4 %collective-permute-done.north = f32[56,8,128]{2,1,0:T(8,128)S(1)} collective-permute-done((f32[56,8,128]{2,1,0:T(8,128)S(1)}, f32[56,8,128]{2,1,0:T(8,128)S(1)}, u32[]{:S(2)}, u32[]{:S(2)}) %collective-permute-start) | collective-permute-done | bytes 229408 | tf_op jit(solution)/shard_map/ppermute | solution.py:583
  26.2 4.6 %collective-permute-done.1.south = f32[56,8,128]{2,1,0:T(8,128)S(1)} collective-permute-done((f32[56,8,128]{2,1,0:T(8,128)S(1)}, f32[56,8,128]{2,1,0:T(8,128)S(1)}, u32[]{:S(2)}, u32[]{:S(2)}) %collective-permute-start.1) | collective-permute-done | bytes 229408 | tf_op jit(solution)/shard_map/ppermute | solution.py:584
  30.9 0.1 collective-permute-start.2
  31.0 3.5 %collective-permute-start.3 = (f32[272,128]{1,0:T(8,128)S(1)}, f32[272,128]{1,0:T(8,128)S(1)}, u32[]{:S(2)}, u32[]{:S(2)}) collective-permute-start(f32[272,128]{1,0:T(8,128)S(1)} %get-tuple-element.16), channel_id=1, source_target_pairs={{1,0},{2,1},{3,2},{4,3},{5,4},{6,5},{7,6},{0,7},{9,8},{10,9},{11,1... | collective-permute-start | bytes 417800 | tf_op jit(solution)/shard_map/ppermute | solution.py:588
  34.5 3.1 %collective-permute-done.2.west = f32[272,128]{1,0:T(8,128)S(1)} collective-permute-done((f32[272,128]{1,0:T(8,128)S(1)}, f32[272,128]{1,0:T(8,128)S(1)}, u32[]{:S(2)}, u32[]{:S(2)}) %collective-permute-start.2) | collective-permute-done | bytes 139296 | tf_op jit(solution)/shard_map/ppermute | solution.py:587
  37.6 8.1 %shard_map.142 = f32[3,16,64,128]{3,2,1,0:T(8,128)} custom-call(f32[3,16,64,128]{3,2,1,0:T(8,128)S(1)} %copy-done.1, f32[56,8,128]{2,1,0:T(8,128)S(1)} %collective-permute-done.north, f32[56,8,128]{2,1,0:T(8,128)S(1)} %collective-permute-done.1.south, f32[272,128]{1,0:T(8,128)S(1)} %collective-permute-done.2.west, ...), custom_call_target="tpu_custom_call" | custom-call | tf_op jit(solution)/shard_map/pallas_call | solution.py:511
  45.7 29.4 %all-gather.2.cloned.1.call-done = f32[3072,128]{1,0:T(8,128)} async-done(((f32[96,128]{1,0:T(8,128)}), f32[3072,128]{1,0:T(8,128)}) %all-gather.2.cloned.1.call-update) | async-done | bytes 1572880 | tf_op jit(solution)/shard_map/all_gather | solution.py:581
  75.1 1.4 %copy-done.2 = f32[3072,128]{1,0:T(8,128)S(1)} copy-done((f32[3072,128]{1,0:T(8,128)S(1)}, f32[3072,128]{1,0:T(8,128)}, u32[]{:S(2)}) %copy-start.2) | copy-done | bytes 1572888
  76.5 2.0 %shard_map.143 = f32[3,4,64,256]{3,2,1,0:T(8,128)} custom-call(f32[4,8,96,128]{3,2,1,0:T(8,128)S(1)} %bitcast.2), custom_call_target="tpu_custom_call" | custom-call | tf_op jit(solution)/shard_map/pallas_call | solution.py:563
  (21 shorter events, 0.1 us)
Async XLA Ops:
  7.2 68.0 %all-gather.2.cloned.1.call-start = ((), (), s32[]{:S(2)}) async-start(), calls=%async_computation | async-start | bytes 1622016 | tf_op jit(solution)/shard_map/all_gather | solution.py:581
  7.2 1.4 %copy-start = (f32[3,16,64,128]{3,2,1,0:T(8,128)S(1)}, f32[3,16,64,128]{3,2,1,0:T(8,128)}, u32[]{:S(2)}) copy-start(f32[3,16,64,128]{3,2,1,0:T(8,128)} %field.3) | copy-start | bytes 4718596
  8.6 0.9 %copy-start.5 = (bf16[768,128]{1,0:T(8,128)(2,1)S(1)}, bf16[768,128]{1,0:T(8,128)(2,1)}, u32[]{:S(2)}) copy-start(bf16[768,128]{1,0:T(8,128)(2,1)} %constant.23.clone.part_columns) | copy-start | bytes 589828
  9.5 0.7 copy-start.12
  10.2 0.7 copy-start.13
  10.9 0.7 copy-start.14
  11.6 25.9 %copy-start.1 = (f32[3,16,64,128]{3,2,1,0:T(8,128)S(1)}, f32[3,16,64,128]{3,2,1,0:T(8,128)}, u32[]{:S(2)}) copy-start(f32[3,16,64,128]{3,2,1,0:T(8,128)} %field.3) | copy-start | bytes 4718596
  11.6 26.0 %copy-start.3 = (bf16[512,256]{1,0:T(8,128)(2,1)S(1)}, bf16[512,256]{1,0:T(8,128)(2,1)}, u32[]{:S(2)}) copy-start(bf16[512,256]{1,0:T(8,128)(2,1)} %constant.31.clone.halo_w) | copy-start | bytes 786436
  11.6 26.0 %copy-start.4 = (bf16[384,256]{1,0:T(8,128)(2,1)S(1)}, bf16[384,256]{1,0:T(8,128)(2,1)}, u32[]{:S(2)}) copy-start(bf16[384,256]{1,0:T(8,128)(2,1)} %constant.32.clone.spread) | copy-start | bytes 589828
  11.6 26.0 %copy-start.6 = (bf16[144,256]{1,0:T(8,128)(2,1)S(1)}, bf16[144,256]{1,0:T(8,128)(2,1)}, u32[]{:S(2)}) copy-start(bf16[144,256]{1,0:T(8,128)(2,1)} %constant.25.clone.forward) | copy-start | bytes 221188
  11.6 26.0 %copy-start.7 = (bf16[256,128]{1,0:T(8,128)(2,1)S(1)}, bf16[256,128]{1,0:T(8,128)(2,1)}, u32[]{:S(2)}) copy-start(bf16[256,128]{1,0:T(8,128)(2,1)} %constant.30.clone.back) | copy-start | bytes 196612
  11.6 26.0 %copy-start.8 = (bf16[256,128]{1,0:T(8,128)(2,1)S(1)}, bf16[256,128]{1,0:T(8,128)(2,1)}, u32[]{:S(2)}) copy-start(bf16[256,128]{1,0:T(8,128)(2,1)} %constant.27.clone.smooth_w) | copy-start | bytes 196612
  11.7 26.0 %copy-start.9 = (bf16[256,128]{1,0:T(8,128)(2,1)S(1)}, bf16[256,128]{1,0:T(8,128)(2,1)}, u32[]{:S(2)}) copy-start(bf16[256,128]{1,0:T(8,128)(2,1)} %constant.26.clone.inverse) | copy-start | bytes 196612
  11.7 26.0 %copy-start.10 = (bf16[128,128]{1,0:T(8,128)(2,1)S(1)}, bf16[128,128]{1,0:T(8,128)(2,1)}, u32[]{:S(2)}) copy-start(bf16[128,128]{1,0:T(8,128)(2,1)} %constant.29.clone.inverse2) | copy-start | bytes 98308
  11.7 26.0 %copy-start.11 = (bf16[128,128]{1,0:T(8,128)(2,1)S(1)}, bf16[128,128]{1,0:T(8,128)(2,1)}, u32[]{:S(2)}) copy-start(bf16[128,128]{1,0:T(8,128)(2,1)} %constant.28.clone.forward2) | copy-start | bytes 98308
  15.9 10.4 %collective-permute-start = (f32[56,8,128]{2,1,0:T(8,128)S(1)}, f32[56,8,128]{2,1,0:T(8,128)S(1)}, u32[]{:S(2)}, u32[]{:S(2)}) collective-permute-start(f32[56,8,128]{2,1,0:T(8,128)S(1)} %get-tuple-element.10), channel_id=1, source_target_pairs={{0,8},{8,16},{16,24},{24,0},{1,9},{9,17},{17,25},{25,1},{2,10},{10... | collective-permute-start | bytes 688136 | tf_op jit(solution)/shard_map/ppermute | solution.py:583
  18.8 12.0 %collective-permute-start.1 = (f32[56,8,128]{2,1,0:T(8,128)S(1)}, f32[56,8,128]{2,1,0:T(8,128)S(1)}, u32[]{:S(2)}, u32[]{:S(2)}) collective-permute-start(f32[56,8,128]{2,1,0:T(8,128)S(1)} %get-tuple-element.11), channel_id=1, source_target_pairs={{8,0},{16,8},{24,16},{0,24},{9,1},{17,9},{25,17},{1,25},{10,2},{18... | collective-permute-start | bytes 688136 | tf_op jit(solution)/shard_map/ppermute | solution.py:584
  30.9 6.7 %collective-permute-start.2 = (f32[272,128]{1,0:T(8,128)S(1)}, f32[272,128]{1,0:T(8,128)S(1)}, u32[]{:S(2)}, u32[]{:S(2)}) collective-permute-start(f32[272,128]{1,0:T(8,128)S(1)} %get-tuple-element.15), channel_id=1, source_target_pairs={{0,1},{1,2},{2,3},{3,4},{4,5},{5,6},{6,7},{7,0},{8,9},{9,10},{10,1... | collective-permute-start | bytes 417800 | tf_op jit(solution)/shard_map/ppermute | solution.py:587
  31.0 6.6 %collective-permute-start.3 = (f32[272,128]{1,0:T(8,128)S(1)}, f32[272,128]{1,0:T(8,128)S(1)}, u32[]{:S(2)}, u32[]{:S(2)}) collective-permute-start(f32[272,128]{1,0:T(8,128)S(1)} %get-tuple-element.16), channel_id=1, source_target_pairs={{1,0},{2,1},{3,2},{4,3},{5,4},{6,5},{7,6},{0,7},{9,8},{10,9},{11,1... | collective-permute-start | bytes 417800 | tf_op jit(solution)/shard_map/ppermute | solution.py:588
  75.1 1.4 %copy-start.2 = (f32[3072,128]{1,0:T(8,128)S(1)}, f32[3072,128]{1,0:T(8,128)}, u32[]{:S(2)}) copy-start(f32[3072,128]{1,0:T(8,128)} %all-gather.2.cloned.1.call-done) | copy-start | bytes 4718596
Sparse Core Ops, SparseCore 0:
  16.0 59.0 all-gather.1

commit v2 on v1

--- a/solution.py
+++ b/solution.py
@@ -143,23 +143,10 @@
         expand[0, j, 16 * j : 16 * j + 16] = 1
         expand[1, j, 64 + 8 * j : 64 + 8 * j + 8] = 1
     w["expand"] = expand
-    twice = {}
-    for k, value in smooth_row(0).items():
-        for y, other in smooth_row(k).items():
-            twice[y] = twice.get(y, 0.0) + value * other
-    columns = np.zeros((NV, 2, 128, 128))
-    for m in range(-1, 34):
-        for t, value in twice.items():
-            if 0 <= 4 * m + t < NL:
-                for v in range(NV):
-                    columns[v, :, 4 * m + t, 40 * v + m + 1] = value
-    w["part_columns"] = columns.reshape(NV * 256, 128)
-    rows = np.zeros((24, 2, 64))
-    for m in range(-1, 18):
-        for t, value in twice.items():
-            if 0 <= 4 * m + t < NR:
-                rows[m % 24, :, 4 * m + t] = value
-    w["part_rows"] = rows.reshape(24, 128)
+    last = np.zeros((256, 128))
+    last[:128, :32] = forward2[:, :32]
+    last[128:, :32] = forward2[:, :32]
+    w["last"] = last
     return {name: as_bf16(matrix) for name, matrix in w.items()}
 
 
@@ -205,7 +192,7 @@
     return even, here + 0.5 * (even + next_even)
 
 
-def pack_kernel(field, masks, expand, part_columns, part_rows, top, bottom, left, right, own_masks, share, wide):
+def pack_kernel(field, masks, expand, top, bottom, left, right, own_masks):
     lane = lax.broadcasted_iota(jnp.int32, (8, NL), 1) // 8
 
     def pack_rows(step, _):
@@ -239,35 +226,18 @@
         out[6] = own_masks[i]
         out[7] = jnp.zeros((8, NL), F32)
 
-    def columns(step, _):
-        planes = pl.ds(step * 4, 4)
-        terms = []
-        for v in range(NV):
-            terms += list(two_terms(field[v, planes].reshape(4 * NR, NL)))
-        wide[planes] = dot(jnp.concatenate(terms, 1), part_columns[...]).reshape(4, NR, NL)
-        return 0
-
-    lax.fori_loop(0, NZ // 4, columns, 0)
-    smooth, _ = lift_planes([wide[z] for z in range(NZ)])
-    smooth, _ = lift_planes(smooth)
-    high, low = two_terms(jnp.concatenate(smooth, 1))
-    part = dot(part_rows[...], jnp.concatenate([high, low], 0))
-    for z in range(4):
-        share[z * 24 : (z + 1) * 24, :] = part[:, z * NL : (z + 1) * NL]
-
 
 def pack(field, masks):
     w = weights()
-    shapes = [(56, 8, NL), (56, 8, NL), (NV, NR, NL), (NV, NR, NL), (2, 8, NL), (96, NL)]
+    shapes = [(56, 8, NL), (56, 8, NL), (NV, NR, NL), (NV, NR, NL), (2, 8, NL)]
     vmem = pl.BlockSpec(memory_space=pltpu.VMEM)
     return pl.pallas_call(
         pack_kernel,
         out_shape=[jax.ShapeDtypeStruct(s, F32) for s in shapes],
-        in_specs=[vmem] * 5,
-        out_specs=[vmem] * 6,
-        scratch_shapes=[pltpu.VMEM((NZ, NR, NL), F32)],
+        in_specs=[vmem] * 3,
+        out_specs=[vmem] * 5,
         compiler_params=pltpu.CompilerParams(vmem_limit_bytes=VMEM_LIMIT),
-    )(field, masks.transpose(0, 2, 3, 1), w["expand"], w["part_columns"], w["part_rows"])
+    )(field, masks.transpose(0, 2, 3, 1), w["expand"])
 
 
 def join_kernel(left, right, own_masks, north, south, to_left, to_right):
@@ -299,8 +269,8 @@
 
 def wave_kernel(
     field, north, south, west, east, own_masks,
-    forward, inverse, smooth_w, forward2, inverse2, back, halo_w, spread,
-    out,
+    forward, inverse, smooth_w, forward2, inverse2, back, halo_w, spread, last,
+    out, share,
     cells, first, halo_x, halo, gain, gain2, low, second, kept2, low_back, kept, sems,
 ):
     copies = []
@@ -421,6 +391,12 @@
     for n in range(4):
         for t in range(3):
             terms = jnp.concatenate(two_terms(second[n, t]), 1)
+            if n == 0 and t < 2:
+                part = dot(terms, last[...]).reshape(NV, 4, 8, NL)
+                for v in range(NV):
+                    share[16 * v + 8 * t : 16 * v + 8 * t + 8, :] = part[v, 0] + sum(
+                        pltpu.roll(part[v, z], 32 * z, 1) for z in range(1, 4)
+                    )
             if t < 2:
                 kept2[n, :, 8 + 8 * t : 16 + 8 * t, :] = dot(terms, gain2[t + 1, n]).reshape(NV * 4, 8, NL)
             else:
@@ -507,12 +483,12 @@
     w = weights()
     vmem = pl.BlockSpec(memory_space=pltpu.VMEM)
     anywhere = pl.BlockSpec(memory_space=pl.ANY)
-    names = ["forward", "inverse", "smooth", "forward2", "inverse2", "back", "halo", "spread"]
+    names = ["forward", "inverse", "smooth", "forward2", "inverse2", "back", "halo", "spread", "last"]
     return pl.pallas_call(
         wave_kernel,
-        out_shape=jax.ShapeDtypeStruct((NV, NZ, NR, NL), F32),
+        out_shape=[jax.ShapeDtypeStruct((NV, NZ, NR, NL), F32), jax.ShapeDtypeStruct((48, NL), F32)],
         in_specs=[anywhere] * 5 + [vmem] * (1 + len(names)),
-        out_specs=vmem,
+        out_specs=[vmem, vmem],
         scratch_shapes=[
             pltpu.VMEM((NV, 21, 96, NL), F32),
             pltpu.VMEM((4, NV * 8, 40, NL), F32),
@@ -532,27 +508,18 @@
 
 
 def coarse_kernel(count_x, count_y, shares, out):
-    lane = lax.broadcasted_iota(jnp.int32, (16, NL), 1)
-    row = lax.broadcasted_iota(jnp.int32, (8, NL), 0)
+    lane = lax.broadcasted_iota(jnp.int32, (16, NL), 1) // 32
 
     def block(i, _):
-        before, after = lax.rem(i + count_x - 1, count_x), lax.rem(i + 1, count_x)
-        for z in range(4):
-            pieces = []
-            for j in range(count_y):
-                first = shares[i, j, 24 * z : 24 * z + 8, :]
-                second = shares[i, j, 24 * z + 8 : 24 * z + 16, :]
-                first += jnp.where(row < 4, shares[before, j, 24 * z + 16 : 24 * z + 24, :], 0.0)
-                second += jnp.where(row < 4, 0.0, shares[after, j, 24 * z + 16 : 24 * z + 24, :])
-                pieces.append(jnp.concatenate([first, second], 0))
-            for v in range(NV):
-                for t in range(count_y // 4):
-                    total = jnp.zeros((16, NL), F32)
-                    for q in range(-1, 5):
-                        start = 32 * q - 1
-                        turned = pltpu.roll(pieces[(4 * t + q) % count_y], (start - 40 * v) % NL, 1)
-                        total += jnp.where((lane >= start) & (lane < start + 35), turned, 0.0)
-                    out[v, z, pl.ds(pl.multiple_of(16 * i, 16), 16), NL * t : NL * (t + 1)] = total
+        rows = pl.ds(pl.multiple_of(16 * i, 16), 16)
+        for v in range(NV):
+            for t in range(count_y // 4):
+                parts = [shares[i, 4 * t + q, 16 * v : 16 * v + 16, :] for q in range(4)]
+                for z in range(4):
+                    turned = [pltpu.roll(p, (32 * (q - z)) % NL, 1) if q != z else p for q, p in enumerate(parts)]
+                    low = jnp.where(lane == 0, turned[0], turned[1])
+                    high = jnp.where(lane == 2, turned[2], turned[3])
+                    out[v, z, rows, NL * t : NL * (t + 1)] = jnp.where(lane < 2, low, high)
         return 0
 
     lax.fori_loop(0, count_x, block, 0)
@@ -566,7 +533,7 @@
         in_specs=[vmem],
         out_specs=vmem,
         compiler_params=pltpu.CompilerParams(vmem_limit_bytes=VMEM_LIMIT),
-    )(shares.reshape(count_x, count_y, 96, NL))
+    )(shares.reshape(count_x, count_y, 48, NL))
 
 
 def shifts(axis):
@@ -577,8 +544,7 @@
 
 def body(field, masks):
     count_x, count_y = lax.axis_size("gx"), lax.axis_size("gy")
-    top, bottom, left, right, own_masks, share = pack(field, masks)
-    shares = lax.all_gather(share, ("gx", "gy"), axis=0, tiled=True)
+    top, bottom, left, right, own_masks = pack(field, masks)
     up, down = shifts("gx")
     north = lax.ppermute(bottom, "gx", up)
     south = lax.ppermute(top, "gx", down)
@@ -586,7 +552,8 @@
     up, down = shifts("gy")
     west = lax.ppermute(to_right, "gy", up)
     east = lax.ppermute(to_left, "gy", down)
-    restored = wave(field, north, south, west, east, own_masks)
+    restored, share = wave(field, north, south, west, east, own_masks)
+    shares = lax.all_gather(share, ("gx", "gy"), axis=0, tiled=True)
     return restored, coarse_of(shares, count_x, count_y)
 
 

time: 85.7 us -> 82.7 us (0.965)
  blocking collectives: 0 us -> 42.3 us
  waiting for transfers between devices: 43.5 us -> 13.6 us
  between operations: 14.2 us -> 0.73 us
  Pallas kernels: 14.2 us -> 12.1 us
    all_gather x0 -> x1, blocking collectives: none -> 42.3 us  [body(): shares = lax.all_gather(share, ('gx', 'gy'), axis=0, tiled=True)]
    all_gather x1 -> x0, waiting for transfers between devices: 29.4 us -> none  [body(): shares = lax.all_gather(share, ('gx', 'gy'), axis=0, tiled=True)]
    pallas_call x1, Pallas kernels: 4.14 us -> 2.22 us  [pack(): pl.pallas_call(pack_kernel, out_shape=[jax.ShapeDtypeStruct(s, F32) for s...]
    unnamed x30 -> x26, local copies, waits for them, and re-layouts: 5.85 us -> 6 us
  transfers between devices with their start and end apart: 5 -> 4, of which waited for: 4 -> 3; matrix products, arithmetic and copies ran while one was open for 0% -> 0% of each run, Pallas kernels for 9% -> 0%
where the time goes in v2:
time: 82.7 us; the launch traced here: 82.2 us
  blocking collectives  42.3 us (51%)
  waiting for transfers between devices  13.6 us (16%)
  Pallas kernels  12.1 us (15%)
  starting transfers between devices  7.5 us (9%)
  local copies, waits for them, and re-layouts  6 us (7%)
    all_gather x1, blocking collectives, body(): shares = lax.all_gather(share, ('gx', 'gy'), axis=0, tiled=True)  42.3 us
    pallas_call x1, Pallas kernels, wave(): pl.pallas_call(wave_kernel, out_shape=[jax.ShapeDtypeStruct((NV, NZ, NR,...  8.08 us
    ppermute x1, waiting for transfers between devices, body(): north = lax.ppermute(bottom, 'gx', up)  6.43 us
    unnamed x26, local copies, waits for them, and re-layouts  6 us
    ppermute x1, waiting for transfers between devices, body(): south = lax.ppermute(top, 'gx', down)  4.34 us
    ppermute x1, starting transfers between devices, body(): east = lax.ppermute(to_left, 'gy', down)  3.53 us
    ppermute x1, starting transfers between devices, body(): north = lax.ppermute(bottom, 'gx', up)  2.96 us
    ppermute x1, waiting for transfers between devices, body(): west = lax.ppermute(to_right, 'gy', up)  2.84 us
  transfers between devices with their start and end apart: 4, of which 3 were waited for; matrix products, arithmetic and copies ran while one was open for 0% of the time, Pallas kernels for 0%

profile of v2, /device:TPU:0, one launch (start us, length us, event | category | flops | bytes accessed | tf_op | source)
XLA Modules:
  0.0 82.2 jit_solution(17500740962688830044)
XLA Ops:
  0.6 0.0 copy-start
  0.6 1.4 %copy-done = f32[3,16,64,128]{3,2,1,0:T(8,128)S(1)} copy-done((f32[3,16,64,128]{3,2,1,0:T(8,128)S(1)}, f32[3,16,64,128]{3,2,1,0:T(8,128)}, u32[]{:S(2)}) %copy-start) | copy-done | bytes 1572888
  2.0 0.7 copy-done.11
  2.7 0.7 copy-done.12
  3.4 0.0 copy-start.5
  3.4 0.0 copy-start.6
  3.5 2.2 %shard_map.131 = (f32[56,8,128]{2,1,0:T(8,128)S(1)}, f32[56,8,128]{2,1,0:T(8,128)S(1)}, f32[3,64,128]{2,1,0:T(8,128)S(1)}, f32[3,64,128]{2,1,0:T(8,128)S(1)}, f32[2,8,128]{2,1,0:T(8,128)S(1)}) custom-call(f32[3,16,64,128]{3,2,1,0:T(8,128)S(1)} %copy-done, s32[2,2,4,7]{3,2,1,0:T(4,128)S(1)} %bitcast.3, bf16[2,4,128]{2,1,0:T(4,128)(2,1)S(1)} %copy-done.12), custom_call_target="tpu_custom_call" | custom-call | tf_op jit(solution)/shard_map/pallas_call | solution.py:234
  5.7 3.0 %collective-permute-start = (f32[56,8,128]{2,1,0:T(8,128)S(1)}, f32[56,8,128]{2,1,0:T(8,128)S(1)}, u32[]{:S(2)}, u32[]{:S(2)}) collective-permute-start(f32[56,8,128]{2,1,0:T(8,128)S(1)} %get-tuple-element.11), channel_id=1, source_target_pairs={{0,8},{8,16},{16,24},{24,0},{1,9},{9,17},{17,25},{25,1},{2,10},{10... | collective-permute-start | bytes 688136 | tf_op jit(solution)/shard_map/ppermute | solution.py:549
  8.6 1.0 %collective-permute-start.1 = (f32[56,8,128]{2,1,0:T(8,128)S(1)}, f32[56,8,128]{2,1,0:T(8,128)S(1)}, u32[]{:S(2)}, u32[]{:S(2)}) collective-permute-start(f32[56,8,128]{2,1,0:T(8,128)S(1)} %get-tuple-element.12), channel_id=1, source_target_pairs={{8,0},{16,8},{24,16},{0,24},{9,1},{17,9},{25,17},{1,25},{10,2},{18... | collective-permute-start | bytes 688136 | tf_op jit(solution)/shard_map/ppermute | solution.py:550
  9.6 6.4 %collective-permute-done.north = f32[56,8,128]{2,1,0:T(8,128)S(1)} collective-permute-done((f32[56,8,128]{2,1,0:T(8,128)S(1)}, f32[56,8,128]{2,1,0:T(8,128)S(1)}, u32[]{:S(2)}, u32[]{:S(2)}) %collective-permute-start) | collective-permute-done | bytes 229408 | tf_op jit(solution)/shard_map/ppermute | solution.py:549
  16.0 4.3 %collective-permute-done.1.south = f32[56,8,128]{2,1,0:T(8,128)S(1)} collective-permute-done((f32[56,8,128]{2,1,0:T(8,128)S(1)}, f32[56,8,128]{2,1,0:T(8,128)S(1)}, u32[]{:S(2)}, u32[]{:S(2)}) %collective-permute-start.1) | collective-permute-done | bytes 229408 | tf_op jit(solution)/shard_map/ppermute | solution.py:550
  20.4 0.1 collective-permute-start.2
  20.4 3.5 %collective-permute-start.3 = (f32[272,128]{1,0:T(8,128)S(1)}, f32[272,128]{1,0:T(8,128)S(1)}, u32[]{:S(2)}, u32[]{:S(2)}) collective-permute-start(f32[272,128]{1,0:T(8,128)S(1)} %get-tuple-element.17), channel_id=1, source_target_pairs={{1,0},{2,1},{3,2},{4,3},{5,4},{6,5},{7,6},{0,7},{9,8},{10,9},{11,1... | collective-permute-start | bytes 417800 | tf_op jit(solution)/shard_map/ppermute | solution.py:554
  24.0 2.8 %collective-permute-done.2.west = f32[272,128]{1,0:T(8,128)S(1)} collective-permute-done((f32[272,128]{1,0:T(8,128)S(1)}, f32[272,128]{1,0:T(8,128)S(1)}, u32[]{:S(2)}, u32[]{:S(2)}) %collective-permute-start.2) | collective-permute-done | bytes 139296 | tf_op jit(solution)/shard_map/ppermute | solution.py:553
  26.8 0.0 collective-permute-done.3.east
  26.8 0.0 copy-done.1
  26.9 0.0 copy-start.7
  26.9 0.8 %copy-done.7 = bf16[256,128]{1,0:T(8,128)(2,1)S(1)} copy-done((bf16[256,128]{1,0:T(8,128)(2,1)S(1)}, bf16[256,128]{1,0:T(8,128)(2,1)}, u32[]{:S(2)}) %copy-start.7) | copy-done | bytes 65560
  27.7 0.8 %copy-done.8 = bf16[256,128]{1,0:T(8,128)(2,1)S(1)} copy-done((bf16[256,128]{1,0:T(8,128)(2,1)S(1)}, bf16[256,128]{1,0:T(8,128)(2,1)}, u32[]{:S(2)}) %copy-start.8) | copy-done | bytes 65560
  28.5 0.8 copy-done.9
  29.3 0.8 copy-done.10
  30.1 8.1 %shard_map.133 = (f32[3,16,64,128]{3,2,1,0:T(8,128)}, f32[48,128]{1,0:T(8,128)S(1)}) custom-call(f32[3,16,64,128]{3,2,1,0:T(8,128)S(1)} %copy-done.1, f32[56,8,128]{2,1,0:T(8,128)S(1)} %collective-permute-done.north, f32[56,8,128]{2,1,0:T(8,128)S(1)} %collective-permute-done.1.south, f32[272,128]{1,0:T(8,128)S(1)} %collective-permute-done.2.west, ...), custom_call_target="tpu_custom_call" | custom-call | tf_op jit(solution)/shard_map/pallas_call | solution.py:487
  38.2 42.3 %all_gather.3 = f32[1536,128]{1,0:T(8,128)S(1)} all-gather(f32[48,128]{1,0:T(8,128)S(1)} %get-tuple-element.19), channel_id=1, replica_groups=mesh['gx'=4,'gy'=8] {'gx','gy'}, dimensions={0}, use_global_device_ids=true | all-gather | bytes 811008 | tf_op jit(solution)/shard_map/all_gather | solution.py:556
  80.4 1.8 %shard_map.134 = f32[3,4,64,256]{3,2,1,0:T(8,128)} custom-call(f32[4,8,48,128]{3,2,1,0:T(8,128)S(1)} %bitcast.2), custom_call_target="tpu_custom_call" | custom-call | tf_op jit(solution)/shard_map/pallas_call | solution.py:530
  (15 shorter events, 0.0 us)
Async XLA Ops:
  0.6 1.4 %copy-start = (f32[3,16,64,128]{3,2,1,0:T(8,128)S(1)}, f32[3,16,64,128]{3,2,1,0:T(8,128)}, u32[]{:S(2)}) copy-start(f32[3,16,64,128]{3,2,1,0:T(8,128)} %field.3) | copy-start | bytes 4718596
  2.0 0.7 copy-start.11
  2.7 0.7 copy-start.12
  3.4 23.4 %copy-start.1 = (f32[3,16,64,128]{3,2,1,0:T(8,128)S(1)}, f32[3,16,64,128]{3,2,1,0:T(8,128)}, u32[]{:S(2)}) copy-start(f32[3,16,64,128]{3,2,1,0:T(8,128)} %field.3) | copy-start | bytes 4718596
  3.4 23.4 %copy-start.2 = (bf16[512,256]{1,0:T(8,128)(2,1)S(1)}, bf16[512,256]{1,0:T(8,128)(2,1)}, u32[]{:S(2)}) copy-start(bf16[512,256]{1,0:T(8,128)(2,1)} %constant.27.clone.halo_w) | copy-start | bytes 786436
  3.4 23.4 %copy-start.3 = (bf16[384,256]{1,0:T(8,128)(2,1)S(1)}, bf16[384,256]{1,0:T(8,128)(2,1)}, u32[]{:S(2)}) copy-start(bf16[384,256]{1,0:T(8,128)(2,1)} %constant.28.clone.spread) | copy-start | bytes 589828
  3.4 23.4 %copy-start.4 = (bf16[144,256]{1,0:T(8,128)(2,1)S(1)}, bf16[144,256]{1,0:T(8,128)(2,1)}, u32[]{:S(2)}) copy-start(bf16[144,256]{1,0:T(8,128)(2,1)} %constant.21.clone.forward) | copy-start | bytes 221188
  3.4 23.4 %copy-start.5 = (bf16[256,128]{1,0:T(8,128)(2,1)S(1)}, bf16[256,128]{1,0:T(8,128)(2,1)}, u32[]{:S(2)}) copy-start(bf16[256,128]{1,0:T(8,128)(2,1)} %constant.29.clone.last) | copy-start | bytes 196612
  3.4 23.4 %copy-start.6 = (bf16[256,128]{1,0:T(8,128)(2,1)S(1)}, bf16[256,128]{1,0:T(8,128)(2,1)}, u32[]{:S(2)}) copy-start(bf16[256,128]{1,0:T(8,128)(2,1)} %constant.26.clone.back) | copy-start | bytes 196612
  5.7 10.3 %collective-permute-start = (f32[56,8,128]{2,1,0:T(8,128)S(1)}, f32[56,8,128]{2,1,0:T(8,128)S(1)}, u32[]{:S(2)}, u32[]{:S(2)}) collective-permute-start(f32[56,8,128]{2,1,0:T(8,128)S(1)} %get-tuple-element.11), channel_id=1, source_target_pairs={{0,8},{8,16},{16,24},{24,0},{1,9},{9,17},{17,25},{25,1},{2,10},{10... | collective-permute-start | bytes 688136 | tf_op jit(solution)/shard_map/ppermute | solution.py:549
  8.6 11.7 %collective-permute-start.1 = (f32[56,8,128]{2,1,0:T(8,128)S(1)}, f32[56,8,128]{2,1,0:T(8,128)S(1)}, u32[]{:S(2)}, u32[]{:S(2)}) collective-permute-start(f32[56,8,128]{2,1,0:T(8,128)S(1)} %get-tuple-element.12), channel_id=1, source_target_pairs={{8,0},{16,8},{24,16},{0,24},{9,1},{17,9},{25,17},{1,25},{10,2},{18... | collective-permute-start | bytes 688136 | tf_op jit(solution)/shard_map/ppermute | solution.py:550
  20.4 6.4 %collective-permute-start.2 = (f32[272,128]{1,0:T(8,128)S(1)}, f32[272,128]{1,0:T(8,128)S(1)}, u32[]{:S(2)}, u32[]{:S(2)}) collective-permute-start(f32[272,128]{1,0:T(8,128)S(1)} %get-tuple-element.16), channel_id=1, source_target_pairs={{0,1},{1,2},{2,3},{3,4},{4,5},{5,6},{6,7},{7,0},{8,9},{9,10},{10,1... | collective-permute-start | bytes 417800 | tf_op jit(solution)/shard_map/ppermute | solution.py:553
  20.4 6.4 %collective-permute-start.3 = (f32[272,128]{1,0:T(8,128)S(1)}, f32[272,128]{1,0:T(8,128)S(1)}, u32[]{:S(2)}, u32[]{:S(2)}) collective-permute-start(f32[272,128]{1,0:T(8,128)S(1)} %get-tuple-element.17), channel_id=1, source_target_pairs={{1,0},{2,1},{3,2},{4,3},{5,4},{6,5},{7,6},{0,7},{9,8},{10,9},{11,1... | collective-permute-start | bytes 417800 | tf_op jit(solution)/shard_map/ppermute | solution.py:554
  26.9 0.8 %copy-start.7 = (bf16[256,128]{1,0:T(8,128)(2,1)S(1)}, bf16[256,128]{1,0:T(8,128)(2,1)}, u32[]{:S(2)}) copy-start(bf16[256,128]{1,0:T(8,128)(2,1)} %constant.23.clone.smooth_w) | copy-start | bytes 196612
  27.7 0.8 %copy-start.8 = (bf16[256,128]{1,0:T(8,128)(2,1)S(1)}, bf16[256,128]{1,0:T(8,128)(2,1)}, u32[]{:S(2)}) copy-start(bf16[256,128]{1,0:T(8,128)(2,1)} %constant.22.clone.inverse) | copy-start | bytes 196612
  28.5 0.8 copy-start.9
  29.3 0.8 copy-start.10
